TPU v7x, 32 devices: a whole 2x2x4 slice. The times are simulated.
32 devices in a mesh: dp: 16 (over z, x, core), seq: 2 (over y).
Axes of the slice: x: 2, y: 2, z: 4, core: 2. Of those that a mesh axis runs over, the one named last changes fastest.
Arguments:
- hidden: bfloat16 [32, 512, 768], P('dp', 'seq'), may hold values from -6 to 6
- encoded: bfloat16 [32, 1024, 768], P('dp', 'seq'), may hold values from -6 to 6
- cotangent: bfloat16 [32, 512, 768], P('dp', 'seq'), may hold values from -6 to 6
- w_self_qkv: bfloat16 [768, 2304], P(('dp', 'seq')), may hold values from -0.21875 to 0.21875
- w_self_out: bfloat16 [768, 768], P(('dp', 'seq')), may hold values from -0.625 to 0.625
- w_cross_q: bfloat16 [768, 768], P(('dp', 'seq')), may hold values from -0.21875 to 0.21875
- w_cross_kv: bfloat16 [768, 1536], P(('dp', 'seq')), may hold values from -0.21875 to 0.21875
- w_cross_out: bfloat16 [768, 768], P(('dp', 'seq')), may hold values from -0.625 to 0.625
- w_ffn_in: bfloat16 [768, 3072], P(('dp', 'seq')), may hold values from -0.21875 to 0.21875
- w_ffn_out: bfloat16 [3072, 768], P(('dp', 'seq')), may hold values from -0.15625 to 0.15625
- norm_gains: float32 [3, 768], replicated, may hold values from 0.5 to 1.5
- bucket_bias_matrix: float32 [32, 12], replicated, may hold values from -4 to 4
- dec_lengths: int32 [32], P('dp'), may hold values from 1 to 512, as said below
- ident_tags: int32 [32, 512], P('dp', 'seq'), may hold values 0 or 1
- ident_mask: int32 [32, 1024], P('dp'), may hold values from 0 to 1, as said below
- bucket_ids: int32 [512, 512], P('seq'), may hold values from 0 to 31, as said below
Outputs:
- block_out: bfloat16 [32, 512, 768], P('dp', 'seq')
- grad_hidden: bfloat16 [32, 512, 768], P('dp', 'seq')
- grad_encoded: bfloat16 [32, 1024, 768], P('dp', 'seq')
- grad_self_qkv: float32 [768, 2304], P(('dp', 'seq'))
- grad_self_out: float32 [768, 768], P(('dp', 'seq'))
- grad_cross_q: float32 [768, 768], P(('dp', 'seq'))
- grad_cross_kv: float32 [768, 1536], P(('dp', 'seq'))
- grad_cross_out: float32 [768, 768], P(('dp', 'seq'))
- grad_ffn_in: float32 [768, 3072], P(('dp', 'seq'))
- grad_ffn_out: float32 [3072, 768], P(('dp', 'seq'))
- grad_gains: float32 [3, 768], replicated
- grad_table: float32 [32, 12], replicated
Inputs may be any that keep to these rules, and one draw needn't show every extreme that they name: `dec_lengths`: in each aligned block of 2 items at least one item has length 512. `ident_mask`: in every aligned run of 8 encoder positions of an item at least one entry is 1. `bucket_ids`: causal T5 buckets (16 exact, then logarithmic up to a distance of 128) of the distance between the token places of the query and the key, 0 where the key's place is after the query's.
All inputs are finite; a program needn't handle non-finite values. No bound on the sum of `ident_tags` on one device may be relied on, other than what follows from the above.
Results may differ from a plain program's by a relative error of at most 0.02.
Values may be sent and summed in bfloat16 or wider, within the bound.
A program may use at most 256 MiB of HBM per device.

v0:
```python
import jax
import jax.numpy as jnp
from jax import lax
from jax.sharding import PartitionSpec as P

epsilon = 1e-06
score_scale = 0.125
masked_score = -1e30
gelu_coeff = 0.7978845608028654
cubic_coeff = 0.044715


def rms_norm(values, gain):
    return values * lax.rsqrt(jnp.mean(values * values, axis=-1, keepdims=True) + epsilon) * gain


def smooth_gelu(values):
    return (
        0.5
        * values
        * (1.0 + jnp.tanh(gelu_coeff * (values + cubic_coeff * values * values * values)))
    )


def matmul(left, right):
    return jnp.dot(left, right, preferred_element_type=jnp.float32)


def contract_rows(left, right):
    return lax.dot_general(
        left, right, (((0,), (0,)), ((), ())), preferred_element_type=jnp.float32
    )


def contract_cols(left, right):
    return lax.dot_general(
        left, right, (((1,), (1,)), ((), ())), preferred_element_type=jnp.float32
    )


def masked_scores(query, keys, bias, mask):
    scores = (
        jnp.einsum("iqhe,ikhe->ihqk", query, keys, preferred_element_type=jnp.float32) * score_scale
    )
    scores = scores + bias
    return jnp.where(mask[:, None], scores, masked_score)


def attend_forward(query, keys, values, bias, mask):
    scores = masked_scores(query, keys, bias, mask)
    top = jnp.max(scores, axis=-1, keepdims=True)
    expo = jnp.exp(scores - top)
    total = jnp.sum(expo, axis=-1, keepdims=True)
    probs = (expo / total).astype(jnp.bfloat16)
    output = jnp.einsum("ihqk,ikhe->iqhe", probs, values, preferred_element_type=jnp.float32)
    return (output.astype(jnp.bfloat16), top + jnp.log(total))


def attend_backward(query, keys, values, bias, mask, log_total, grad_out):
    probs = jnp.exp(masked_scores(query, keys, bias, mask) - log_total)
    grad_probs = jnp.einsum("iqhe,ikhe->ihqk", grad_out, values, preferred_element_type=jnp.float32)
    grad_values = jnp.einsum(
        "ihqk,iqhe->ikhe", probs.astype(jnp.bfloat16), grad_out, preferred_element_type=jnp.float32
    )
    inner = jnp.sum(grad_probs * probs, axis=-1, keepdims=True)
    grad_scores = (probs * (grad_probs - inner)).astype(jnp.bfloat16)
    grad_query = (
        jnp.einsum("ihqk,ikhe->iqhe", grad_scores, keys, preferred_element_type=jnp.float32)
        * score_scale
    )
    grad_keys = (
        jnp.einsum("ihqk,iqhe->ikhe", grad_scores, query, preferred_element_type=jnp.float32)
        * score_scale
    )
    return (grad_query, grad_keys, grad_values, grad_scores)


def body(
    hidden,
    encoded,
    cotangent,
    w_self_qkv,
    w_self_out,
    w_cross_q,
    w_cross_kv,
    w_cross_out,
    w_ffn_in,
    w_ffn_out,
    norm_gains,
    bucket_bias_matrix,
    dec_lengths,
    ident_tags,
    ident_mask,
    bucket_ids,
):
    items, local_dec, width = hidden.shape
    local_enc = encoded.shape[1]
    heads = bucket_bias_matrix.shape[1]
    head_dim = width // heads
    bucket_count = bucket_bias_matrix.shape[0]
    full_dec = local_dec * lax.axis_size("seq")
    full_enc = local_enc * lax.axis_size("seq")
    device_count = lax.axis_size("dp") * lax.axis_size("seq")
    query_pos = lax.axis_index("seq") * local_dec + jnp.arange(local_dec)
    key_pos = jnp.arange(full_dec)
    self_mask = (key_pos[None, None, :] <= query_pos[None, :, None]) & (
        key_pos[None, None, :] < dec_lengths[:, None, None]
    )
    cross_mask = (ident_tags[:, :, None] == 0) | (ident_mask[:, None, :] == 1)
    bucket_indicator = (bucket_ids[None, :, :] == jnp.arange(bucket_count)[:, None, None]).astype(
        jnp.float32
    )
    self_attention_bias = jnp.einsum(
        "ufp,uo->ofp", bucket_indicator, bucket_bias_matrix, precision=lax.Precision.HIGHEST
    )
    inputs = hidden.reshape(-1, width).astype(jnp.float32)
    enc_rows = encoded.reshape(-1, width)

    def forward_pass(weights):
        wqkv, wso, wcq, wckv, wco, win, wout = weights
        normed = rms_norm(inputs, norm_gains[0]).astype(jnp.bfloat16)
        qkv = matmul(normed, wqkv).astype(jnp.bfloat16)
        query = qkv[:, :width].reshape(items, local_dec, heads, head_dim)
        local_kv = qkv[:, width:].reshape(items, local_dec, 2 * width)
        all_kv = lax.all_gather(local_kv, "seq", axis=1, tiled=True)
        keys = all_kv[:, :, :width].reshape(items, full_dec, heads, head_dim)
        values = all_kv[:, :, width:].reshape(items, full_dec, heads, head_dim)
        attended, self_lse = attend_forward(query, keys, values, self_attention_bias, self_mask)
        attended = attended.reshape(-1, width)
        after_self = inputs + matmul(attended, wso)
        normed_two = rms_norm(after_self, norm_gains[1]).astype(jnp.bfloat16)
        local_cq = matmul(normed_two, wcq).astype(jnp.bfloat16)
        local_ckv = matmul(enc_rows, wckv).astype(jnp.bfloat16).reshape(items, local_enc, 2 * width)
        cross_query = local_cq.reshape(items, local_dec, heads, head_dim)
        all_ckv = lax.all_gather(local_ckv, "seq", axis=1, tiled=True)
        cross_keys = all_ckv[:, :, :width].reshape(items, full_enc, heads, head_dim)
        cross_values = all_ckv[:, :, width:].reshape(items, full_enc, heads, head_dim)
        cross_att, cross_lse = attend_forward(
            cross_query, cross_keys, cross_values, 0.0, cross_mask
        )
        cross_att = cross_att.reshape(-1, width)
        after_cross = after_self + matmul(cross_att, wco)
        normed_three = rms_norm(after_cross, norm_gains[2]).astype(jnp.bfloat16)
        pre = matmul(normed_three, win)
        act = smooth_gelu(pre).astype(jnp.bfloat16)
        result = after_cross + matmul(act, wout)
        return dict(
            normed=normed,
            qkv=qkv,
            query=query,
            keys=keys,
            values=values,
            attended=attended,
            self_lse=self_lse,
            after_self=after_self,
            normed_two=normed_two,
            cross_query=cross_query,
            cross_keys=cross_keys,
            cross_values=cross_values,
            cross_att=cross_att,
            cross_lse=cross_lse,
            cross_part_mask=cross_mask,
            after_cross=after_cross,
            normed_three=normed_three,
            pre=pre,
            act=act,
            result=result,
        )

    shards = (w_self_qkv, w_self_out, w_cross_q, w_cross_kv, w_cross_out, w_ffn_in, w_ffn_out)
    first = (
        lax.all_gather(shards[0], ("dp", "seq"), axis=0, tiled=True),
        lax.all_gather(shards[1], ("dp", "seq"), axis=0, tiled=True),
        lax.all_gather(shards[2], ("dp", "seq"), axis=0, tiled=True),
        lax.all_gather(shards[3], ("dp", "seq"), axis=0, tiled=True),
        lax.all_gather(shards[4], ("dp", "seq"), axis=0, tiled=True),
        lax.all_gather(shards[5], ("dp", "seq"), axis=0, tiled=True),
        lax.all_gather(shards[6], ("dp", "seq"), axis=0, tiled=True),
    )
    state = forward_pass(first)
    output = state["result"]
    weights = first
    weights = (
        lax.all_gather(shards[0], ("dp", "seq"), axis=0, tiled=True),
        lax.all_gather(shards[1], ("dp", "seq"), axis=0, tiled=True),
        lax.all_gather(shards[2], ("dp", "seq"), axis=0, tiled=True),
        lax.all_gather(shards[3], ("dp", "seq"), axis=0, tiled=True),
        lax.all_gather(shards[4], ("dp", "seq"), axis=0, tiled=True),
        lax.all_gather(shards[5], ("dp", "seq"), axis=0, tiled=True),
        lax.all_gather(shards[6], ("dp", "seq"), axis=0, tiled=True),
    )
    state = forward_pass(weights)
    wqkv, wso, wcq, wckv, wco, win, wout = weights
    grad_top = cotangent.reshape(-1, width).astype(jnp.float32)
    grad_low = grad_top.astype(jnp.bfloat16)
    grad_wout = contract_rows(state["act"], grad_low)
    grad_act = contract_cols(grad_low, wout)
    grad_pre = jax.vjp(smooth_gelu, state["pre"])[1](grad_act)[0].astype(jnp.bfloat16)
    grad_win = contract_rows(state["normed_three"], grad_pre)
    normalized_gradient = contract_cols(grad_pre, win)
    norm_back, gain_three = jax.vjp(rms_norm, state["after_cross"], norm_gains[2])[1](
        normalized_gradient
    )
    cross_attention_gradient = grad_top + norm_back
    cross_low = cross_attention_gradient.astype(jnp.bfloat16)
    grad_wco = contract_rows(state["cross_att"], cross_low)
    grad_catt_local = contract_cols(cross_low, wco).astype(jnp.bfloat16)
    grad_catt = grad_catt_local.reshape(items, local_dec, heads, head_dim)
    grad_cq, grad_ck, grad_cv, unused_scores = attend_backward(
        state["cross_query"],
        state["cross_keys"],
        state["cross_values"],
        0.0,
        cross_mask,
        state["cross_lse"],
        grad_catt,
    )
    grad_ckv_terms = jnp.concatenate(
        [grad_ck.reshape(items, full_enc, width), grad_cv.reshape(items, full_enc, width)], axis=-1
    )
    grad_ckv = lax.psum_scatter(
        grad_ckv_terms.astype(jnp.bfloat16), "seq", scatter_dimension=1, tiled=True
    ).reshape(-1, 2 * width)
    grad_cq_low = grad_cq.reshape(-1, width).astype(jnp.bfloat16)
    grad_wckv = contract_rows(enc_rows, grad_ckv)
    grad_enc = contract_cols(grad_ckv, wckv).astype(jnp.bfloat16).reshape(encoded.shape)
    grad_wcq = contract_rows(state["normed_two"], grad_cq_low)
    second_normalized_gradient = contract_cols(grad_cq_low, wcq)
    norm_back_two, gain_two = jax.vjp(rms_norm, state["after_self"], norm_gains[1])[1](
        second_normalized_gradient
    )
    grad_self = cross_attention_gradient + norm_back_two
    self_low = grad_self.astype(jnp.bfloat16)
    grad_wso = contract_rows(state["attended"], self_low)
    grad_att = (
        contract_cols(self_low, wso).astype(jnp.bfloat16).reshape(items, local_dec, heads, head_dim)
    )
    grad_q, grad_k, grad_v, grad_scores = attend_backward(
        state["query"],
        state["keys"],
        state["values"],
        self_attention_bias,
        self_mask,
        state["self_lse"],
        grad_att,
    )
    score_totals = jnp.sum(grad_scores.astype(jnp.float32), axis=0)
    bias_gradient = jnp.einsum(
        "xru,pru->xp", bucket_indicator, score_totals, precision=lax.Precision.HIGHEST
    )
    grad_kv_terms = jnp.concatenate(
        [grad_k.reshape(items, full_dec, width), grad_v.reshape(items, full_dec, width)], axis=-1
    )
    grad_kv = lax.psum_scatter(
        grad_kv_terms.astype(jnp.bfloat16), "seq", scatter_dimension=1, tiled=True
    ).reshape(-1, 2 * width)
    grad_qkv = jnp.concatenate([grad_q.reshape(-1, width).astype(jnp.bfloat16), grad_kv], axis=-1)
    grad_wqkv = contract_rows(state["normed"], grad_qkv)
    grad_normed_one = contract_cols(grad_qkv, wqkv)
    norm_back_one, gain_one = jax.vjp(rms_norm, inputs, norm_gains[0])[1](grad_normed_one)
    grad_inputs = (grad_self + norm_back_one).astype(jnp.bfloat16).reshape(hidden.shape)
    full_terms = (grad_wqkv, grad_wso, grad_wcq, grad_wckv, grad_wco, grad_win, grad_wout)
    tiled = tuple((term.reshape(8 * device_count, -1) for term in full_terms))
    summed = (
        lax.psum_scatter(tiled[0], ("dp", "seq"), scatter_dimension=0, tiled=True),
        lax.psum_scatter(tiled[1], ("dp", "seq"), scatter_dimension=0, tiled=True),
        lax.psum_scatter(tiled[2], ("dp", "seq"), scatter_dimension=0, tiled=True),
        lax.psum_scatter(tiled[3], ("dp", "seq"), scatter_dimension=0, tiled=True),
        lax.psum_scatter(tiled[4], ("dp", "seq"), scatter_dimension=0, tiled=True),
        lax.psum_scatter(tiled[5], ("dp", "seq"), scatter_dimension=0, tiled=True),
        lax.psum_scatter(tiled[6], ("dp", "seq"), scatter_dimension=0, tiled=True),
    )
    summed = tuple((piece.reshape(-1, term.shape[1]) for piece, term in zip(summed, full_terms)))
    gain_grads, table_grads = lax.psum(
        (jnp.stack([gain_one, gain_two, gain_three]), bias_gradient), ("dp", "seq")
    )
    block_out = output.astype(jnp.bfloat16).reshape(hidden.shape)
    return (
        block_out,
        grad_inputs,
        grad_enc,
        summed[0],
        summed[1],
        summed[2],
        summed[3],
        summed[4],
        summed[5],
        summed[6],
        gain_grads,
        table_grads,
    )


def solution(mesh):
    placed = (
        P("dp", "seq", None),
        P("dp", "seq", None),
        P("dp", "seq", None),
        P(("dp", "seq"), None),
        P(("dp", "seq"), None),
        P(("dp", "seq"), None),
        P(("dp", "seq"), None),
        P(("dp", "seq"), None),
        P(("dp", "seq"), None),
        P(("dp", "seq"), None),
        P(),
        P(),
        P("dp"),
        P("dp", "seq"),
        P("dp", None),
        P("seq", None),
    )
    return jax.shard_map(
        body,
        mesh=mesh,
        in_specs=placed,
        out_specs=(
            P("dp", "seq", None),
            P("dp", "seq", None),
            P("dp", "seq", None),
            P(("dp", "seq"), None),
            P(("dp", "seq"), None),
            P(("dp", "seq"), None),
            P(("dp", "seq"), None),
            P(("dp", "seq"), None),
            P(("dp", "seq"), None),
            P(("dp", "seq"), None),
            P(),
            P(),
        ),
        check_vma=False,
    )
```

profile of v0, /device:TPU:0, one launch (start us, length us, event | category | flops | bytes accessed | tf_op | source)
XLA Modules:
  0.0 1649.3 jit_solution(2035033114883546000)
XLA Ops:
  13.1 60.7 %all-gather.10.cloned.1.call-done = bf16[768,2304]{1,0:T(8,128)(2,1)} async-done(((bf16[24,2304]{1,0:T(8,128)(2,1)}), bf16[768,2304]{1,0:T(8,128)(2,1)}) %all-gather.10.cloned.1.call-update) | async-done | bytes 3538960 | tf_op jit(solution)/shard_map/all_gather | solution.py:172
  81.1 51.9 %all-gather.16.cloned.1.call-done = bf16[768,1536]{1,0:T(8,128)(2,1)} async-done(((bf16[24,1536]{1,0:T(8,128)(2,1)}), bf16[768,1536]{1,0:T(8,128)(2,1)}) %all-gather.16.cloned.1.call-update) | async-done | bytes 2359312 | tf_op jit(solution)/shard_map/all_gather | solution.py:175
  155.3 43.2 %all-gather.26.cloned.1.call-done = bf16[3072,768]{1,0:T(8,128)(2,1)} async-done(((bf16[96,768]{1,0:T(8,128)(2,1)}), bf16[3072,768]{1,0:T(8,128)(2,1)}) %all-gather.26.cloned.1.call-update) | async-done | bytes 4718608 | tf_op jit(solution)/shard_map/all_gather | solution.py:178
  207.0 37.2 %all-gather.12.cloned.1.call-done = bf16[2,512,1536]{2,1,0:T(8,128)(2,1)} async-done(((bf16[2,256,1536]{2,1,0:T(8,128)(2,1)}), bf16[2,512,1536]{2,1,0:T(8,128)(2,1)}) %all-gather.12.cloned.1.call-update) | async-done | bytes 3145744 | tf_op jit(solution)/shard_map/all_gather | solution.py:125
  269.2 31.9 %all-gather.14.cloned.1.call-done = bf16[768,768]{1,0:T(8,128)(2,1)} async-done(((bf16[24,768]{1,0:T(8,128)(2,1)}), bf16[768,768]{1,0:T(8,128)(2,1)}) %all-gather.14.cloned.1.call-update) | async-done | bytes 1179664 | tf_op jit(solution)/shard_map/all_gather | solution.py:173
  303.8 53.2 %all-gather.20.cloned.1.call-done = bf16[768,768]{1,0:T(8,128)(2,1)} async-done(((bf16[24,768]{1,0:T(8,128)(2,1)}), bf16[768,768]{1,0:T(8,128)(2,1)}) %all-gather.20.cloned.1.call-update) | async-done | bytes 1179664 | tf_op jit(solution)/shard_map/all_gather | solution.py:174
  365.3 72.6 %all-gather.18.cloned.1.call-done = bf16[2,1024,1536]{2,1,0:T(8,128)(2,1)} async-done(((bf16[2,512,1536]{2,1,0:T(8,128)(2,1)}), bf16[2,1024,1536]{2,1,0:T(8,128)(2,1)}) %all-gather.18.cloned.1.call-update) | async-done | bytes 6291472 | tf_op jit(solution)/shard_map/all_gather | solution.py:135
  453.3 12.5 fusion.10
  465.8 12.0 fusion
  477.9 11.7 fusion.47
  498.0 62.6 %all-gather.24.cloned.1.call-done = bf16[768,3072]{1,0:T(8,128)(2,1)} async-done(((bf16[24,3072]{1,0:T(8,128)(2,1)}), bf16[768,3072]{1,0:T(8,128)(2,1)}) %all-gather.24.cloned.1.call-update) | async-done | bytes 4718608 | tf_op jit(solution)/shard_map/all_gather | solution.py:177
  560.6 12.5 fusion.17
  585.0 19.4 %multiply_reduce_fusion = (f32[2,12,256]{2,1,0:T(8,128)S(1)}, f32[2,12,256,1024]{3,2,1,0:T(8,128)}) fusion(f32[2,12,256]{2,1,0:T(8,128)S(1)} %log_add_fusion.1, f32[2,12,256,1024]{3,2,1,0:T(8,128)} %get-tuple-element.34, pred[2,256,1024]{2,1,0:T(8,128)(4,1)} %broadcast_or_fusion, bf16[2,1024,12,64]{1,3,2,0:T(8,128)(2,1)} %bitcast.141, ...), kind=kOutput, calls=%fused_computation.1 | convolution fusion | flops 836757504 | bytes 54837248 | tf_op jit(solution)/shard_map/iqhe,ikhe->ihqk/dot_general | solution.py:61
  604.4 22.4 %multiply_convert_fusion = bf16[2,12,256,1024]{3,2,1,0:T(8,128)(2,1)} fusion(f32[2,12,256,1024]{3,2,1,0:T(8,128)} %get-tuple-element.41, f32[2,12,256]{2,1,0:T(8,128)S(1)} %get-tuple-element.40, f32[2,12,256]{2,1,0:T(8,128)S(1)} %log_add_fusion.1, f32[2,12,256,1024]{3,2,1,0:T(8,128)} %get-tuple-element.34, pred[2,256,1024]{2,1,0:T(8,128)(4,1)} %broadcast_or_fusion), kind=kLoop, calls=%fused_computation | loop fusion | flops 37748736 | bytes 63488000 | tf_op jit(solution)/shard_map/convert_element_type | solution.py:66
  654.9 9.5 multiply_reduce_fusion.1
  666.9 12.8 convert_reduce_fusion
  689.2 14.6 fusion.25
  708.5 8.9 multiply_convert_fusion.2
  758.2 11.0 reshape.338
  769.3 10.0 fusion.81
  779.3 10.6 reshape.340
  806.1 8.7 reshape.328
  834.4 12.9 fusion.49
  847.4 8.9 add_convert_fusion
  856.3 58.9 %reduce-scatter.22.cloned.1.call-done = f32[8,2304]{1,0:T(8,128)} async-done(((f32[256,2304]{1,0:T(8,128)}), f32[8,2304]{1,0:T(8,128)}) %reduce-scatter.22.cloned.1.call-update) | async-done | bytes 73744 | tf_op jit(solution)/shard_map/reduce_scatter | solution.py:269
  916.8 102.7 %reduce-scatter.18.cloned.1.call-done = f32[8,2304]{1,0:T(8,128)} async-done(((f32[256,2304]{1,0:T(8,128)}), f32[8,2304]{1,0:T(8,128)}) %reduce-scatter.18.cloned.1.call-update) | async-done | bytes 73744 | tf_op jit(solution)/shard_map/reduce_scatter | solution.py:267
  1021.0 101.7 %reduce-scatter.16.cloned.1.call-done = f32[8,2304]{1,0:T(8,128)} async-done(((f32[256,2304]{1,0:T(8,128)}), f32[8,2304]{1,0:T(8,128)}) %reduce-scatter.16.cloned.1.call-update) | async-done | bytes 73744 | tf_op jit(solution)/shard_map/reduce_scatter | solution.py:266
  1130.5 40.7 %all-reduce = (f32[3,768]{1,0:T(4,128)}, f32[32,12]{0,1:T(8,128)}) all-reduce(f32[3,768]{1,0:T(4,128)S(1)} %pad_maximum_fusion.5, f32[32,12]{0,1:T(8,128)S(1)} %fusion.49), channel_id=1, replica_groups=mesh['dp'=16,'seq'=2] {'dp','seq'}, use_global_device_ids=true, to_apply=%region_24.25 | all-reduce | flops 2688 | bytes 21504 | tf_op jit(solution)/shard_map/psum | solution.py:274
  1174.2 89.7 %reduce-scatter.24.cloned.1.call-done = f32[8,9216]{1,0:T(8,128)} async-done(((f32[256,9216]{1,0:T(8,128)}), f32[8,9216]{1,0:T(8,128)}) %reduce-scatter.24.cloned.1.call-update) | async-done | bytes 294928 | tf_op jit(solution)/shard_map/reduce_scatter | solution.py:270
  1265.7 138.8 %reduce-scatter.26.cloned.1.call-done = f32[8,9216]{1,0:T(8,128)} async-done(((f32[256,9216]{1,0:T(8,128)}), f32[8,9216]{1,0:T(8,128)}) %reduce-scatter.26.cloned.1.call-update) | async-done | bytes 294928 | tf_op jit(solution)/shard_map/reduce_scatter | solution.py:271
  1412.6 116.3 %reduce-scatter.14.cloned.1.call-done = f32[8,6912]{1,0:T(8,128)} async-done(((f32[256,6912]{1,0:T(8,128)}), f32[8,6912]{1,0:T(8,128)}) %reduce-scatter.14.cloned.1.call-update) | async-done | bytes 221200 | tf_op jit(solution)/shard_map/reduce_scatter | solution.py:265
  1530.6 110.0 %reduce-scatter.20.cloned.1.call-done = f32[8,4608]{1,0:T(8,128)} async-done(((f32[256,4608]{1,0:T(8,128)}), f32[8,4608]{1,0:T(8,128)}) %reduce-scatter.20.cloned.1.call-update) | async-done | bytes 147472 | tf_op jit(solution)/shard_map/reduce_scatter | solution.py:268
  (215 shorter events, 263.7 us)
Async XLA Ops:
  7.2 125.8 %copy-start = (bf16[2,512,768]{2,1,0:T(8,128)(2,1)S(1)}, bf16[2,512,768]{2,1,0:T(8,128)(2,1)}, u32[]{:S(2)}) copy-start(bf16[2,512,768]{2,1,0:T(8,128)(2,1)} %param.17) | copy-start | bytes 4718596
  7.2 66.7 %all-gather.10.cloned.1.call-start = ((), (), s32[]{:S(2)}) async-start(), calls=%async_computation.9 | async-start | bytes 3649536 | tf_op jit(solution)/shard_map/all_gather | solution.py:172
  7.9 125.0 %all-gather.16.cloned.1.call-start = ((), (), s32[]{:S(2)}) async-start(), calls=%async_computation.12 | async-start | bytes 2433024 | tf_op jit(solution)/shard_map/all_gather | solution.py:175
  8.7 189.8 %all-gather.26.cloned.1.call-start = ((), (), s32[]{:S(2)}) async-start(), calls=%async_computation.17 | async-start | bytes 4866048 | tf_op jit(solution)/shard_map/all_gather | solution.py:178
  9.4 234.8 %all-gather.12.cloned.1.call-start = ((), (), s32[]{:S(2)}) async-start(), calls=%async_computation.10 | async-start | bytes 4718592 | tf_op jit(solution)/shard_map/all_gather | solution.py:125
  10.9 67.0 %copy-start.27 = (f32[512]{0:T(512)}, f32[512]{0:T(512)S(1)}, u32[]{:S(2)}) copy-start(f32[512]{0:T(512)S(1)} %rsqrt.36) | copy-start | bytes 6148
  11.7 66.1 %copy-start.25 = (f32[768]{0:T(1024)}, f32[768]{0:T(1024)S(1)}, u32[]{:S(2)}) copy-start(f32[768]{0:T(1024)S(1)} %get-tuple-element.19) | copy-start | bytes 9220
  13.1 64.7 %copy-start.19 = (bf16[512,768]{1,0:T(8,128)(2,1)}, bf16[512,768]{1,0:T(8,128)(2,1)S(1)}, u32[]{:S(2)}) copy-start(bf16[512,768]{1,0:T(8,128)(2,1)S(1)} %fusion.37) | copy-start | bytes 2359300
  79.8 221.3 %all-gather.14.cloned.1.call-start = ((), (), s32[]{:S(2)}) async-start(), calls=%async_computation.11 | async-start | bytes 1216512 | tf_op jit(solution)/shard_map/all_gather | solution.py:173
  80.4 276.6 %all-gather.20.cloned.1.call-start = ((), (), s32[]{:S(2)}) async-start(), calls=%async_computation.14 | async-start | bytes 1216512 | tf_op jit(solution)/shard_map/all_gather | solution.py:174
  81.0 356.9 %all-gather.18.cloned.1.call-start = ((), (), s32[]{:S(2)}) async-start(), calls=%async_computation.13 | async-start | bytes 9437184 | tf_op jit(solution)/shard_map/all_gather | solution.py:135
  138.6 356.4 %all-gather.22.cloned.1.call-start = ((), (), s32[]{:S(2)}) async-start(), calls=%async_computation.15 | async-start | bytes 1216512 | tf_op jit(solution)/shard_map/all_gather | solution.py:176
  139.4 421.2 %all-gather.24.cloned.1.call-start = ((), (), s32[]{:S(2)}) async-start(), calls=%async_computation.16 | async-start | bytes 4866048 | tf_op jit(solution)/shard_map/all_gather | solution.py:177
  140.1 659.3 %reduce-scatter.10.cloned.1.call-start = ((), (), s32[]{:S(2)}) async-start(), calls=%async_computation.18 | async-start | bytes 4718592 | tf_op jit(solution)/shard_map/reduce_scatter | solution.py:254
  249.7 8.5 copy-start.10
  303.8 61.5 %copy-start.4 = (f32[512,768]{1,0:T(8,128)}, f32[512,768]{1,0:T(8,128)S(1)}, u32[]{:S(2)}) copy-start(f32[512,768]{1,0:T(8,128)S(1)} %get-tuple-element.32) | copy-start | bytes 4718596
  465.8 12.0 copy-start.12
  560.6 12.5 copy-start.36
  604.4 22.5 %copy-start.3 = (bf16[2,1024,768]{1,2,0:T(8,128)(2,1)S(1)}, bf16[2,1024,768]{1,2,0:T(8,128)(2,1)}, u32[]{:S(2)}) copy-start(bf16[2,1024,768]{1,2,0:T(8,128)(2,1)} %copy.77) | copy-start | bytes 9437188
  666.9 12.8 copy-start.15
  689.2 125.7 %reduce-scatter.12.cloned.1.call-start = ((), (), s32[]{:S(2)}) async-start(), calls=%async_computation.19 | async-start | bytes 9437184 | tf_op jit(solution)/shard_map/reduce_scatter | solution.py:221
  728.1 187.1 %reduce-scatter.22.cloned.1.call-start = ((), (), s32[]{:S(2)}) async-start(), calls=%async_computation.24 | async-start | bytes 2433024 | tf_op jit(solution)/shard_map/reduce_scatter | solution.py:269
  735.4 284.1 %reduce-scatter.18.cloned.1.call-start = ((), (), s32[]{:S(2)}) async-start(), calls=%async_computation.22 | async-start | bytes 2433024 | tf_op jit(solution)/shard_map/reduce_scatter | solution.py:267
  743.1 379.6 %reduce-scatter.16.cloned.1.call-start = ((), (), s32[]{:S(2)}) async-start(), calls=%async_computation.21 | async-start | bytes 2433024 | tf_op jit(solution)/shard_map/reduce_scatter | solution.py:266
  750.8 513.2 %reduce-scatter.24.cloned.1.call-start = ((), (), s32[]{:S(2)}) async-start(), calls=%async_computation.25 | async-start | bytes 9732096 | tf_op jit(solution)/shard_map/reduce_scatter | solution.py:270
  769.2 635.2 %reduce-scatter.26.cloned.1.call-start = ((), (), s32[]{:S(2)}) async-start(), calls=%async_computation.26 | async-start | bytes 9732096 | tf_op jit(solution)/shard_map/reduce_scatter | solution.py:271
  789.8 739.1 %reduce-scatter.14.cloned.1.call-start = ((), (), s32[]{:S(2)}) async-start(), calls=%async_computation.20 | async-start | bytes 7299072 | tf_op jit(solution)/shard_map/reduce_scatter | solution.py:265
  814.8 825.9 %reduce-scatter.20.cloned.1.call-start = ((), (), s32[]{:S(2)}) async-start(), calls=%async_computation.23 | async-start | bytes 4866048 | tf_op jit(solution)/shard_map/reduce_scatter | solution.py:268
  847.3 276.9 %copy-start.26 = (f32[768]{0:T(1024)S(1)}, f32[768]{0:T(1024)}, u32[]{:S(2)}) copy-start(f32[768]{0:T(1024)} %copy-done.25) | copy-start | bytes 9220
  847.3 276.9 %copy-start.28 = (f32[512]{0:T(512)S(1)}, f32[512]{0:T(512)}, u32[]{:S(2)}) copy-start(f32[512]{0:T(512)} %copy-done.27) | copy-start | bytes 6148
  1124.2 47.0 %copy-start.30 = (f32[1,2,2,128]{3,1,2,0:T(2,128)S(1)}, f32[1,2,2,128]{3,1,2,0:T(2,128)}, u32[]{:S(2)}) copy-start(f32[1,2,2,128]{3,1,2,0:T(2,128)} %copy-done.29) | copy-start | bytes 6148
  1124.2 47.0 %copy-start.7 = (f32[512,768]{1,0:T(8,128)S(1)}, f32[512,768]{1,0:T(8,128)}, u32[]{:S(2)}) copy-start(f32[512,768]{1,0:T(8,128)} %copy-done.6) | copy-start | bytes 4718596
  (26 other events, 78.2 us)
Sparse Core Ops, SparseCore 0:
  10.9 62.8 all-gather.9
  76.8 56.1 all-gather.15
  135.9 62.5 all-gather.25
  200.4 43.7 all-gather.11
  247.0 54.1 all-gather.13
  303.9 53.0 all-gather.19
  358.6 79.3 all-gather.17
  440.8 54.1 all-gather.21
  497.9 62.5 all-gather.23
  689.3 42.1 reduce-scatter.9
  733.9 77.0 reduce-scatter.11
  816.2 99.0 reduce-scatter.21
  921.4 98.0 reduce-scatter.17
  1024.6 98.0 reduce-scatter.15
  1129.4 134.4 reduce-scatter.23
  1269.7 134.7 reduce-scatter.25
  1410.9 117.9 reduce-scatter.13
  1534.3 106.3 reduce-scatter.19
where the time goes:
time: 1660 us; the launch traced here: 1650 us
  waiting for transfers between devices  1140 us (69%)
  matrix products  241 us (15%)
  local copies, waits for them, and re-layouts  144 us (9%)
  other arithmetic  68.4 us (4%)
  blocking collectives  40.7 us (2%)
    reduce_scatter x1, waiting for transfers between devices, body(): lax.psum_scatter(tiled[6], ('dp', 'seq'), scatter_dimension=0, tiled=True)  139 us
    reduce_scatter x1, waiting for transfers between devices, body(): lax.psum_scatter(tiled[0], ('dp', 'seq'), scatter_dimension=0, tiled=True)  116 us
    reduce_scatter x1, waiting for transfers between devices, body(): lax.psum_scatter(tiled[3], ('dp', 'seq'), scatter_dimension=0, tiled=True)  110 us
    reduce_scatter x1, waiting for transfers between devices, body(): lax.psum_scatter(tiled[2], ('dp', 'seq'), scatter_dimension=0, tiled=True)  103 us
    reduce_scatter x1, waiting for transfers between devices, body(): lax.psum_scatter(tiled[1], ('dp', 'seq'), scatter_dimension=0, tiled=True)  102 us
    reduce_scatter x1, waiting for transfers between devices, body(): lax.psum_scatter(tiled[5], ('dp', 'seq'), scatter_dimension=0, tiled=True)  89.7 us
    all_gather x1, waiting for transfers between devices, forward_pass(): all_ckv = lax.all_gather(local_ckv, 'seq', axis=1, tiled=True)  72.6 us
    all_gather x1, waiting for transfers between devices, body(): lax.all_gather(shards[5], ('dp', 'seq'), axis=0, tiled=True)  62.6 us
  transfers between devices with their start and end apart: 18, of which 16 were waited for; matrix products, arithmetic and copies ran while one was open for 19% of the time, Pallas kernels for 0%

commit v1 on v0

--- a/solution.py
+++ b/solution.py
@@ -1,6 +1,12 @@
+import functools
+import itertools
+import typing
+
 import jax
 import jax.numpy as jnp
 from jax import lax
+from jax.experimental import pallas as pl
+from jax.experimental.pallas import tpu as pltpu
 from jax.sharding import PartitionSpec as P
 
 epsilon = 1e-06
@@ -75,7 +81,7 @@
     return (grad_query, grad_keys, grad_values, grad_scores)
 
 
-def body(
+def split_body(
     hidden,
     encoded,
     cotangent,
@@ -291,6 +297,1404 @@
     )
 
 
+pair = 128
+
+
+def nt(left, right):
+    return lax.dot_general(left, right, (((1,), (1,)), ((), ())), preferred_element_type=jnp.float32)
+
+
+masked_bucket = pair - 1
+
+
+def half_masks():
+    lane = lax.broadcasted_iota(jnp.int32, (1, pair), 1)
+    low = (lane < pair // 2).astype(jnp.float32).astype(jnp.bfloat16)
+    high = (lane >= pair // 2).astype(jnp.float32).astype(jnp.bfloat16)
+    return (low, high)
+
+
+def look_up(row, ids):
+    spread = jnp.broadcast_to(row, (ids.shape[0], pair))
+    pieces = [
+        jnp.take_along_axis(spread, ids[:, at : at + pair], axis=1, mode="promise_in_bounds")
+        for at in range(0, ids.shape[1], pair)
+    ]
+    return jnp.concatenate(pieces, axis=1)
+
+
+def store_lse(lse_ref, columns):
+    lane = lax.broadcasted_iota(jnp.int32, (columns[0].shape[0], pair), 1)
+    both = jnp.where(lane == 0, columns[0], columns[1])
+    lse_ref[...] = jnp.transpose(both)[: lse_ref.shape[0]]
+
+
+def attend_rows(scores, values):
+    top = jnp.max(scores, axis=1, keepdims=True)
+    expo = jnp.exp(scores - top)
+    total = jnp.sum(expo, axis=1, keepdims=True)
+    output = matmul(expo.astype(jnp.bfloat16), values)
+    return output / total, top + jnp.log(total)
+
+
+def self_forward_kernel(q_ref, k_ref, v_ref, ids_ref, table_ref, att_ref, full_ref, lse_ref, *, block):
+    rows = q_ref.shape[0]
+    low, high = half_masks()
+    lane = lax.broadcasted_iota(jnp.int32, (block, pair), 1)
+    columns = ([], [])
+    for start in range(0, rows, block):
+        span = start + block
+        here = slice(start, span)
+        query = q_ref[here, :] * jnp.bfloat16(score_scale)
+        outs = []
+        for side, mask in enumerate((low, high)):
+            scores = nt(query * mask, k_ref[:span, :])
+            scores = scores + look_up(table_ref[0, side : side + 1, :], ids_ref[here, :span])
+            output, lse = attend_rows(scores, v_ref[:span, :])
+            outs.append(output)
+            columns[side].append(lse)
+        both = jnp.where(lane < pair // 2, outs[0], outs[1])
+        full_ref[here, :] = both
+        att_ref[here, :] = both.astype(jnp.bfloat16)
+    store_lse(lse_ref, [jnp.concatenate(column, axis=0) for column in columns])
+
+
+def cross_forward_kernel(q_ref, k_ref, v_ref, tag_ref, mark_ref, att_ref, full_ref, lse_ref, *, block):
+    rows = q_ref.shape[0]
+    low, high = half_masks()
+    lane = lax.broadcasted_iota(jnp.int32, (block, pair), 1)
+    keys = [k_ref[...] * mask + mark_ref[...] * other for mask, other in ((low, high), (high, low))]
+    columns = ([], [])
+    for start in range(0, rows, block):
+        here = slice(start, start + block)
+        query = q_ref[here, :] * jnp.bfloat16(score_scale)
+        outs = []
+        for side, (mask, other) in enumerate(((low, high), (high, low))):
+            scores = nt(query * mask + tag_ref[here, :] * other, keys[side])
+            output, lse = attend_rows(scores, v_ref[...])
+            outs.append(output)
+            columns[side].append(lse)
+        both = jnp.where(lane < pair // 2, outs[0], outs[1])
+        full_ref[here, :] = both
+        att_ref[here, :] = both.astype(jnp.bfloat16)
+    store_lse(lse_ref, [jnp.concatenate(column, axis=0) for column in columns])
+
+
+def inner_rows(grad_ref, full_ref):
+    product = jnp.transpose(grad_ref[...].astype(jnp.float32) * full_ref[...])
+    half = pair // 2
+    return [jnp.sum(product[at : at + half], axis=0, keepdims=True) for at in (0, half)]
+
+
+def backward_chunk(key, key_t, value, query, query_ext, grad, lse, inner, bias):
+    scores = nt(key, query_ext)
+    if bias is not None:
+        scores = scores + bias
+    probs = jnp.exp(scores - lse)
+    grad_probs = nt(value, grad)
+    grad_scores = (probs * (grad_probs - inner)).astype(jnp.bfloat16)
+    grad_value = matmul(probs.astype(jnp.bfloat16), grad)
+    grad_key = matmul(grad_scores, query)
+    grad_query_t = matmul(key_t, grad_scores)
+    return grad_scores, grad_value, grad_key, grad_query_t
+
+
+def rms_rows(values, gain):
+    scale = lax.rsqrt(jnp.mean(values * values, axis=1, keepdims=True) + epsilon)
+    return (values * scale * gain).astype(jnp.bfloat16)
+
+
+class Given(typing.NamedTuple):
+    length: typing.Any
+    ids: typing.Any
+    tag: typing.Any
+    mark: typing.Any
+    table: typing.Any
+    gains: typing.Any
+    x: typing.Any
+    wqkv: typing.Any
+
+
+class Fetched(typing.NamedTuple):
+    enc: typing.Any
+    wso: typing.Any
+    wcq: typing.Any
+    wckv: typing.Any
+    wco: typing.Any
+
+
+class Kept(typing.NamedTuple):
+    n1: typing.Any
+    ids_t: typing.Any
+    qkv: typing.Any
+    att: typing.Any
+    sfull: typing.Any
+    x1: typing.Any
+    n2: typing.Any
+    cq: typing.Any
+    ckv: typing.Any
+    catt: typing.Any
+    cfull: typing.Any
+    x2: typing.Any
+    n3: typing.Any
+
+
+def attention_forward_kernel(*refs, pairs, block):
+    refs = list(refs)
+
+    def take(kind):
+        taken = kind(*refs[: len(kind._fields)])
+        del refs[: len(kind._fields)]
+        return taken
+
+    given, distant, kept = take(Given), take(Fetched), take(Kept)
+    slse_ref, clse_ref = refs[:2]
+    del refs[:2]
+    here, near = take(Kept), take(Fetched)
+    masked, fetch_sem, keep_sem = refs
+    made, wanted = Kept(*range(len(here))), Fetched(*range(len(near)))
+    at = pl.program_id(0)
+    rows, width = here.att.shape
+
+    def lanes(index):
+        return pl.ds(pl.multiple_of(index * pair, pair), pair)
+
+    def columns(panel):
+        return slice(panel * width, (panel + 1) * width)
+
+    def fetch(i):
+        return pltpu.make_async_copy(distant[i], near[i], fetch_sem.at[i])
+
+    def ship(i):
+        return pltpu.make_async_copy(here[i], kept[i], keep_sem.at[i])
+
+    @pl.when(at == 0)
+    def _():
+        for i in wanted:
+            fetch(i).start()
+        gain = given.gains[0:1, :]
+        for start in range(0, rows, block):
+            rest = slice(start, start + block)
+            here.n1[rest, :] = rms_rows(given.x[rest, :].astype(jnp.float32), gain)
+            for wide in range(0, rows, block):
+                query = lax.broadcasted_iota(jnp.int32, (block, block), 0) + start
+                key = lax.broadcasted_iota(jnp.int32, (block, block), 1) + wide
+                keep = (key <= query) & (key < given.length[0:1, :])
+                ids = given.ids[rest, wide : wide + block].astype(jnp.float32)
+                ids = jnp.where(keep, ids, float(masked_bucket))
+                masked[rest, wide : wide + block] = ids.astype(jnp.int32)
+                here.ids_t[wide : wide + block, rest] = jnp.transpose(ids).astype(jnp.int32)
+        ship(made.n1).start()
+        ship(made.ids_t).start()
+
+    @pl.when(at == 1)
+    def _():
+        for panel in range(3):
+            product_rows(here.n1, given.wqkv.at[:, columns(panel)], here.qkv.at[:, columns(panel)], 2 * block)
+        ship(made.qkv).start()
+
+    @pl.when((at > 1) & (at <= pairs + 1))
+    def _():
+        index = at - 2
+        self_forward_kernel(
+            here.qkv.at[:, lanes(index)],
+            here.qkv.at[:, lanes(pairs + index)],
+            here.qkv.at[:, lanes(2 * pairs + index)],
+            masked,
+            given.table.at[pl.ds(index, 1)],
+            here.att.at[:, lanes(index)],
+            here.sfull.at[:, lanes(index)],
+            slse_ref,
+            block=block,
+        )
+
+    @pl.when(at == pairs + 2)
+    def _():
+        fetch(wanted.wso).wait()
+        fetch(wanted.wcq).wait()
+        for start in range(0, rows, 2 * block):
+            rest = slice(start, start + 2 * block)
+            total = given.x[rest, :].astype(jnp.float32) + matmul(here.att[rest, :], near.wso[...])
+            here.x1[rest, :] = total
+            here.n2[rest, :] = rms_rows(total, given.gains[1:2, :])
+        product_rows(here.n2, near.wcq, here.cq, 2 * block)
+        for i in (made.att, made.sfull, made.x1, made.n2, made.cq):
+            ship(i).start()
+
+    @pl.when(at == pairs + 3)
+    def _():
+        fetch(wanted.enc).wait()
+        fetch(wanted.wckv).wait()
+        for panel in range(2):
+            product_rows(near.enc, near.wckv.at[:, columns(panel)], here.ckv.at[:, columns(panel)], 2 * block)
+        ship(made.ckv).start()
+
+    @pl.when((at > pairs + 3) & (at <= 2 * pairs + 3))
+    def _():
+        index = at - pairs - 4
+        cross_forward_kernel(
+            here.cq.at[:, lanes(index)],
+            here.ckv.at[:, lanes(index)],
+            here.ckv.at[:, lanes(pairs + index)],
+            given.tag,
+            given.mark,
+            here.catt.at[:, lanes(index)],
+            here.cfull.at[:, lanes(index)],
+            clse_ref,
+            block=block,
+        )
+
+    @pl.when(at == 2 * pairs + 4)
+    def _():
+        ship(made.catt).start()
+        ship(made.cfull).start()
+        fetch(wanted.wco).wait()
+        for start in range(0, rows, 2 * block):
+            rest = slice(start, start + 2 * block)
+            total = here.x1[rest, :] + matmul(here.catt[rest, :], near.wco[...])
+            here.x2[rest, :] = total
+            here.n3[rest, :] = rms_rows(total, given.gains[2:3, :])
+        ship(made.x2).start()
+        ship(made.n3).start()
+        for i in made:
+            ship(i).wait()
+
+
+def cross_backward_pair(q_ref, k_ref, v_ref, tag_ref, mark_ref, grad_ref, full_ref, lse_ref, query_t, *, block, put):
+    low, high = half_masks()
+    inner = inner_rows(grad_ref, full_ref)
+    query = q_ref[...] * jnp.bfloat16(score_scale)
+    queries = [query * low, query * high]
+    exts = [queries[0] + tag_ref[...] * high, queries[1] + tag_ref[...] * low]
+    grads = [grad_ref[...] * low, grad_ref[...] * high]
+    for start in range(0, k_ref.shape[0], block):
+        here = slice(start, start + block)
+        key = k_ref[here, :]
+        parts = [None, None, None]
+        for side, (mask, other) in enumerate(((low, high), (high, low))):
+            own = key * mask
+            _, *news = backward_chunk(
+                own + mark_ref[here, :] * other,
+                jnp.transpose(own),
+                v_ref[here, :],
+                queries[side],
+                exts[side],
+                grads[side],
+                lse_ref[side : side + 1, :],
+                inner[side],
+                None,
+            )
+            parts = [new if part is None else part + new for part, new in zip(parts, news)]
+        put(2, here, parts[0].astype(jnp.bfloat16))
+        put(1, here, parts[1].astype(jnp.bfloat16))
+        query_t[...] = parts[2] if start == 0 else query_t[...] + parts[2]
+    put(0, slice(None), (jnp.transpose(query_t[...]) * score_scale).astype(jnp.bfloat16))
+
+
+def self_backward_pair(q_ref, k_ref, v_ref, ids_ref, table_ref, grad_ref, full_ref, lse_ref, ds_ref, query_t, *, block, put):
+    low, high = half_masks()
+    inner = inner_rows(grad_ref, full_ref)
+    query = q_ref[...] * jnp.bfloat16(score_scale)
+    for start in range(0, k_ref.shape[0], block):
+        here = slice(start, start + block)
+        key = k_ref[here, :]
+        parts = [None, None, None]
+        for side, mask in enumerate((low, high)):
+            own = query[start:, :] * mask
+            scores, *news = backward_chunk(
+                key,
+                jnp.transpose(key * mask),
+                v_ref[here, :],
+                own,
+                own,
+                grad_ref[start:, :] * mask,
+                lse_ref[side : side + 1, start:],
+                inner[side][:, start:],
+                look_up(table_ref[0, side : side + 1, :], ids_ref[here, start:]),
+            )
+            ds_ref[side, here, start:] = scores
+            parts = [new if part is None else part + new for part, new in zip(parts, news)]
+        put(2, here, parts[0].astype(jnp.bfloat16))
+        put(1, here, parts[1].astype(jnp.bfloat16))
+        if start == 0:
+            query_t[...] = parts[2]
+        else:
+            query_t[:, start:] += parts[2]
+    put(0, slice(None), (jnp.transpose(query_t[...]) * score_scale).astype(jnp.bfloat16))
+
+
+def rms_back_rows(values, gain, grad):
+    scale = lax.rsqrt(jnp.mean(values * values, axis=1, keepdims=True) + epsilon)
+    weighted = grad * gain
+    inner = jnp.mean(values * weighted, axis=1, keepdims=True)
+    back = scale * weighted - values * (scale * scale * scale * inner)
+    return back, jnp.sum(grad * values * scale, axis=0, keepdims=True)
+
+
+def turn(source, target):
+    rows, columns = source.shape
+    for start in range(0, columns, pair):
+        target[start : start + pair, :rows] = jnp.transpose(source[:, start : start + pair])
+
+
+def product_rows(left, right, target, block, dims=(((1,), (0,)), ((), ()))):
+    for start in range(0, target.shape[0], block):
+        here = slice(start, start + block)
+        product = lax.dot_general(left[here, :], right[...], dims, preferred_element_type=jnp.float32)
+        target[here, :] = product.astype(jnp.bfloat16)
+
+
+nt_dims = (((1,), (1,)), ((), ()))
+
+
+def attention_backward_kernel(
+    cq_ref,
+    ck_ref,
+    cv_ref,
+    tag_ref,
+    mark_ref,
+    gcatt_ref,
+    cfull_ref,
+    clse_ref,
+    q_ref,
+    k_ref,
+    v_ref,
+    ids_ref,
+    table_ref,
+    sfull_ref,
+    slse_ref,
+    gains_ref,
+    x_ref,
+    x1_ref,
+    gx2_ref,
+    n1_ref,
+    n2_ref,
+    att_ref,
+    enc_ref,
+    wcq_ref,
+    wso_ref,
+    wckv_ref,
+    wqkv_ref,
+    ds_ref,
+    gwqkv_ref,
+    gwckv_ref,
+    gwcq_ref,
+    gwso_ref,
+    enc_items,
+    x_items,
+    ggain_ref,
+    gcq,
+    gckv,
+    gqkv,
+    gx1,
+    low_x1,
+    gatt,
+    total,
+    tall,
+    query_t,
+    genc,
+    gx,
+    *swap_sems,
+    pairs,
+    block,
+):
+    enc_sems, x_sems = swap_sems[:3], swap_sems[3:]
+    at = pl.program_id(0)
+    rows, width = gcq.shape
+    keys = gckv.shape[0]
+
+    def lanes(first, index):
+        return pl.ds(pl.multiple_of(first + index * pair, pair), pair)
+
+    @pl.when(at < pairs)
+    def _():
+        def put(kind, where, values):
+            if kind == 0:
+                gcq[where, lanes(0, at)] = values
+            else:
+                gckv[where, lanes((kind - 1) * width, at)] = values
+
+        cross_backward_pair(
+            cq_ref, ck_ref, cv_ref, tag_ref, mark_ref, gcatt_ref, cfull_ref, clse_ref, query_t, block=2 * block, put=put
+        )
+
+    @pl.when(at == pairs)
+    def _():
+        gain = gains_ref[1:2, :]
+        sums = None
+        for start in range(0, rows, block):
+            here = slice(start, start + block)
+            back, part = rms_back_rows(x1_ref[here, :], gain, nt(gcq[here, :], wcq_ref[...]))
+            gx1[here, :] = gx2_ref[here, :] + back
+            low_x1[here, :] = gx1[here, :].astype(jnp.bfloat16)
+            sums = part if sums is None else sums + part
+        ggain_ref[1:2, :] = sums
+        product_rows(low_x1, wso_ref, gatt, 2 * block, nt_dims)
+
+    enc_pieces, x_pieces = enc_sems[1].shape[0], x_sems[1].shape[0]
+    enc_swap = LateSwap(genc, enc_items, enc_sems, enc_pieces)
+    x_swap = LateSwap(gx, x_items, x_sems, x_pieces)
+
+    @pl.when(at == pairs + 1)
+    def _():
+        product_rows(gckv, wckv_ref, genc, 2 * block, nt_dims)
+
+    for piece in range(enc_pieces):
+        pl.when(at == min(pairs + 2 + piece, 2 * pairs + 5))(functools.partial(enc_swap.begin, piece))
+
+    @pl.when((at > pairs + 1) & (at <= 2 * pairs + 1))
+    def _():
+        index = at - pairs - 2
+
+        def put(kind, where, values):
+            gqkv[where, lanes(kind * width, index)] = values
+
+        self_backward_pair(
+            q_ref,
+            k_ref,
+            v_ref,
+            ids_ref,
+            table_ref,
+            gatt.at[:, lanes(0, index)],
+            sfull_ref,
+            slse_ref,
+            ds_ref,
+            query_t,
+            block=block,
+            put=put,
+        )
+
+    @pl.when(at == 2 * pairs + 2)
+    def _():
+        turn(n1_ref, tall)
+
+    for panel in range(3):
+
+        @pl.when(at == 2 * pairs + 2 + panel)
+        def _(panel=panel):
+            columns = slice(panel * width, (panel + 1) * width)
+            product_rows(tall.at[:, :rows], gqkv.at[:, columns], gwqkv_ref, 2 * block)
+            for start in range(0, rows, 2 * block):
+                here = slice(start, start + 2 * block)
+                part = nt(gqkv[here, columns], wqkv_ref[...])
+                total[here, :] = part if panel == 0 else total[here, :] + part
+
+    @pl.when(at == 2 * pairs + 4)
+    def _():
+        gain = gains_ref[0:1, :]
+        sums = None
+        for start in range(0, rows, block):
+            here = slice(start, start + block)
+            back, part = rms_back_rows(x_ref[here, :].astype(jnp.float32), gain, total[here, :])
+            gx[here, :] = (gx1[here, :] + back).astype(jnp.bfloat16)
+            sums = part if sums is None else sums + part
+        ggain_ref[0:1, :] = sums
+        for piece in range(x_pieces):
+            x_swap.begin(piece)
+
+    @pl.when(at == 2 * pairs + 5)
+    def _():
+        turn(enc_ref, tall)
+        for panel in range(2):
+            columns = slice(panel * width, (panel + 1) * width)
+            product_rows(tall.at[:, :keys], gckv.at[:, columns], gwckv_ref.at[:, columns], 2 * block)
+
+    @pl.when(at == 2 * pairs + 6)
+    def _():
+        turn(n2_ref, tall)
+        product_rows(tall.at[:, :rows], gcq, gwcq_ref, 2 * block)
+        turn(att_ref, tall)
+        product_rows(tall.at[:, :rows], low_x1, gwso_ref, 2 * block)
+        enc_swap.finish()
+        x_swap.finish()
+
+
+def table_kernel(gains_ref, ids_ref, ds_ref, out_ref, sums, spread, table, total, came, send, recv, *, buckets):
+    heads, block = ds_ref.shape[0], ds_ref.shape[1]
+
+    @pl.when(pl.program_id(0) == 0)
+    def _():
+        sums[...] = jnp.zeros_like(sums)
+
+    spread[...] = ds_ref[...].astype(jnp.float32)
+    ids = ids_ref[...]
+
+    def step(bucket, carry):
+        chosen = ids == bucket
+        for head in range(heads):
+            picked = jnp.where(chosen, spread[head], 0.0).reshape(block // 8, 8, pair)
+            sums[bucket, head] += jnp.sum(picked, axis=0)
+        return carry
+
+    lax.fori_loop(0, buckets, step, 0)
+
+
+def table_finish(gains_ref, ids_ref, ds_ref, out_ref, sums, spread, table, total, came, send, recv):
+    heads = ds_ref.shape[0]
+
+    def fill():
+        table[...] = jnp.zeros_like(table)
+        table[:, :heads] = jnp.sum(jnp.sum(sums[...], axis=3), axis=2)
+        total[0] = jnp.concatenate([gains_ref[...], table[...]], axis=0)
+
+    def finish():
+        out_ref[...] = total[4]
+
+    return reduce_steps(fill, total, came, send, recv, finish)
+
+
+def block_of(rows, first=0):
+    return pl.BlockSpec((rows, pair), lambda at: (0, first + at))
+
+
+def whole(shape):
+    return pl.BlockSpec(shape, lambda at: (0,) * len(shape))
+
+
+def attention_forward(length, ids, tag_lanes, mark_lanes, table, gains, states, wqkv, enc, wso, wcq, wckv, wco, moves):
+    rows, width = states.shape
+    keys = enc.shape[0]
+    pairs = width // pair
+    low, high = jnp.bfloat16, jnp.float32
+    shapes = Kept(
+        n1=((rows, width), low),
+        ids_t=((rows, rows), jnp.int32),
+        qkv=((rows, 3 * width), low),
+        att=((rows, width), low),
+        sfull=((rows, width), high),
+        x1=((rows, width), high),
+        n2=((rows, width), low),
+        cq=((rows, width), low),
+        ckv=((keys, 2 * width), low),
+        catt=((rows, width), low),
+        cfull=((rows, width), high),
+        x2=((rows, width), high),
+        n3=((rows, width), low),
+    )
+
+    def once(values):
+        return pl.BlockSpec(values.shape, lambda at: (0,) * len(values.shape), pipeline_mode=pl.Buffered(1))
+
+    anywhere = pl.BlockSpec(memory_space=pl.ANY)
+    given = (length, ids, tag_lanes, mark_lanes, table, gains, states, wqkv)
+    distant = (enc, wso, wcq, wckv, wco)
+    outs, moved = carried(
+        functools.partial(attention_forward_kernel, pairs=pairs, block=128),
+        moves,
+        grid=(2 * pairs + 5,),
+        in_specs=[*(once(values) for values in given), *(anywhere for _ in distant)],
+        out_specs=[anywhere] * len(shapes)
+        + [
+            pl.BlockSpec((8, rows), lambda at: (jnp.clip(at - 2, 0, pairs - 1), 0)),
+            pl.BlockSpec((8, rows), lambda at: (jnp.clip(at - pairs - 4, 0, pairs - 1), 0)),
+        ],
+        out_shape=[jax.ShapeDtypeStruct(*shape) for shape in shapes]
+        + [jax.ShapeDtypeStruct((pairs * 8, rows), high)] * 2,
+        scratch_shapes=[pltpu.VMEM(*shape) for shape in shapes]
+        + [pltpu.VMEM(values.shape, values.dtype) for values in distant]
+        + [
+            pltpu.VMEM((rows, rows), jnp.int32),
+            pltpu.SemaphoreType.DMA((len(distant),)),
+            pltpu.SemaphoreType.DMA((len(shapes),)),
+        ],
+        ident=1,
+        name="attention_forward",
+        tail=2,
+    )(*given, *distant)
+    return Kept(*outs[: len(shapes)]), outs[len(shapes) :], moved
+
+
+def deliver_kernel(*refs):
+    count = len(refs) // 3
+    sems = refs[-1]
+    incoming = [pltpu.make_async_copy(refs[i], refs[2 * count + i], sems.at[i]) for i in range(count)]
+    outgoing = [pltpu.make_async_copy(refs[2 * count + i], refs[count + i], sems.at[i]) for i in range(count)]
+    for copy in incoming:
+        copy.start()
+    for one, other in zip(incoming, outgoing):
+        one.wait()
+        other.start()
+    for copy in outgoing:
+        copy.wait()
+
+
+def deliver(results):
+    anywhere = pl.BlockSpec(memory_space=pl.ANY)
+    return pl.pallas_call(
+        deliver_kernel,
+        in_specs=[anywhere] * len(results),
+        out_specs=[anywhere] * len(results),
+        out_shape=[jax.ShapeDtypeStruct(result.shape, result.dtype) for result in results],
+        scratch_shapes=[pltpu.VMEM(result.shape, result.dtype) for result in results]
+        + [pltpu.SemaphoreType.DMA((len(results),))],
+        compiler_params=pltpu.CompilerParams(vmem_limit_bytes=32 * 1024 * 1024),
+        name="deliver",
+    )(*results)
+
+
+def attention_backward(
+    query, ckv, tag_lanes, mark_lanes, grad_catt, cross_full, cross_lse,
+    qkv, ids_t, table, self_full, self_lse,
+    gains, states, after_self, grad_cross, normed, normed_two, attended, enc_rows,
+    wcq, wso, wckv, wqkv, moves,
+):
+    rows, width = query.shape
+    keys = ckv.shape[0]
+    pairs = width // pair
+    last = pairs - 1
+
+    def cross_block(count, first=0):
+        return pl.BlockSpec((count, pair), lambda at: (0, first + jnp.minimum(at, last)))
+
+    def self_index(at):
+        return jnp.clip(at - pairs - 2, 0, last)
+
+    def self_block(count, first=0):
+        return pl.BlockSpec((count, pair), lambda at: (0, first + self_index(at)))
+
+    def once(values):
+        return pl.BlockSpec(values.shape, lambda at: (0,) * len(values.shape), pipeline_mode=pl.Buffered(1))
+
+    def panel(count):
+        return pl.BlockSpec((count, width), lambda at: (0, jnp.clip(at - 2 * pairs - 2, 0, 2)))
+
+    low = jnp.bfloat16
+    wholes = [(width, 2 * width), (width, width), (width, width)]
+    items = [(2, keys // 2, width), (2, rows // 2, width)]
+    return carried(
+        functools.partial(attention_backward_kernel, pairs=pairs, block=128),
+        moves,
+        grid=(2 * pairs + 7,),
+        in_specs=[
+            cross_block(rows),
+            cross_block(keys),
+            cross_block(keys, pairs),
+            once(tag_lanes),
+            once(mark_lanes),
+            cross_block(rows),
+            cross_block(rows),
+            pl.BlockSpec((8, rows), lambda at: (jnp.minimum(at, last), 0)),
+            self_block(rows),
+            self_block(rows, pairs),
+            self_block(rows, 2 * pairs),
+            once(ids_t),
+            pl.BlockSpec((1, 2, pair), lambda at: (self_index(at), 0, 0)),
+            self_block(rows),
+            pl.BlockSpec((8, rows), lambda at: (self_index(at), 0)),
+            *(
+                once(values)
+                for values in (gains, states, after_self, grad_cross, normed, normed_two, attended, enc_rows, wcq, wso, wckv)
+            ),
+            panel(width),
+        ],
+        out_specs=[
+            pl.BlockSpec((2, rows, rows), lambda at: (self_index(at), 0, 0)),
+            panel(width),
+            *(pl.BlockSpec(shape, lambda at: (0, 0), pipeline_mode=pl.Buffered(1)) for shape in wholes),
+            *(pl.BlockSpec(memory_space=pl.ANY) for _ in items),
+            pl.BlockSpec((8, width), lambda at: (0, 0)),
+        ],
+        out_shape=[
+            jax.ShapeDtypeStruct((pairs * 2, rows, rows), low),
+            jax.ShapeDtypeStruct((width, 3 * width), low),
+            *(jax.ShapeDtypeStruct(shape, low) for shape in wholes + items),
+            jax.ShapeDtypeStruct((8, width), jnp.float32),
+        ],
+        scratch_shapes=[
+            pltpu.VMEM((rows, width), low),
+            pltpu.VMEM((keys, 2 * width), low),
+            pltpu.VMEM((rows, 3 * width), low),
+            pltpu.VMEM((rows, width), jnp.float32),
+            pltpu.VMEM((rows, width), low),
+            pltpu.VMEM((rows, width), low),
+            pltpu.VMEM((rows, width), jnp.float32),
+            pltpu.VMEM((width, keys), low),
+            pltpu.VMEM((pair, rows), jnp.float32),
+            pltpu.VMEM((keys, width), low),
+            pltpu.VMEM((rows, width), low),
+            *(pltpu.SemaphoreType.DMA((count,)) for count in (1, 8, 8, 1, 2, 2)),
+        ],
+        ident=3,
+        name="attention_backward",
+        tail=0,
+    )(
+        query, ckv, ckv, tag_lanes, mark_lanes, grad_catt, cross_full, cross_lse,
+        qkv, qkv, qkv, ids_t, table, self_full, self_lse,
+        gains, states, after_self, grad_cross, normed, normed_two, attended, enc_rows,
+        wcq, wso, wckv, wqkv,
+    )
+
+
+def table_sums(gains, ids_t, grad_scores, buckets, moves):
+    heads = grad_scores.shape[0]
+    side = ids_t.shape[0] // pair
+    starts = [sum(side - row for row in range(before)) for before in range(1, side)]
+
+    def place(at):
+        row, column = 0, at
+        for back, start in enumerate(starts):
+            past = jnp.where(at >= start, 1, 0)
+            row = row + past
+            column = column - past * (side - 1 - back)
+        return row, column
+
+    small = (gains.shape[0] + buckets, pair)
+    return carried(
+        functools.partial(table_kernel, buckets=buckets),
+        moves,
+        grid=(side * (side + 1) // 2,),
+        in_specs=[
+            whole(gains.shape),
+            pl.BlockSpec((pair, pair), place),
+            pl.BlockSpec((heads, pair, pair), lambda at: (0, *place(at))),
+        ],
+        out_specs=[whole(small)],
+        out_shape=[jax.ShapeDtypeStruct(small, jnp.float32)],
+        scratch_shapes=[
+            pltpu.VMEM((buckets, heads, 8, pair), jnp.float32),
+            pltpu.VMEM((heads, pair, pair), jnp.float32),
+            pltpu.VMEM((buckets, pair), jnp.float32),
+            pltpu.VMEM((5,) + small, jnp.float32),
+            pltpu.VMEM((6,) + small, jnp.float32),
+            pltpu.SemaphoreType.DMA((6,)),
+            pltpu.SemaphoreType.DMA((6,)),
+        ],
+        ident=5,
+        name="table_sums",
+        last=table_finish,
+        tail=9,
+    )(gains, ids_t, grad_scores)
+
+
+def bring(moves):
+    return carried(
+        None, moves, grid=(1,), in_specs=[], out_specs=[], out_shape=[], scratch_shapes=[], ident=0, name="bring"
+    )()[1]
+
+
+MESH = pl.DeviceIdType.MESH
+grid_z, grid_x, grid_core, grid_y = 4, 2, 2, 2
+kept_slots = 3
+lag = 2
+swap_rows = 128
+block_grid = (grid_z, grid_x, grid_core, grid_y)
+
+
+def position():
+    at = lax.axis_index("dp")
+    return at // 4, (at // 2) % 2, at % 2, lax.axis_index("seq")
+
+
+def device_at(z, x, core, y):
+    return ((z * grid_x + x) * grid_core + core, y)
+
+
+def partners():
+    z, x, core, y = position()
+    along = [device_at((z + step) % grid_z, x, core, y) for step in range(1, grid_z)]
+    return along + [device_at(z, 1 - x, core, y), device_at(z, x, core, 1 - y), device_at(z, x, 1 - core, y)]
+
+
+def meet():
+    barrier = pltpu.get_barrier_semaphore()
+    others = partners()
+    for other in others:
+        pl.semaphore_signal(barrier, inc=1, device_id=other, device_id_type=MESH)
+    pl.semaphore_wait(barrier, len(others))
+
+
+def remote(source, target, send, recv, other):
+    return pltpu.make_async_remote_copy(
+        src_ref=source, dst_ref=target, send_sem=send, recv_sem=recv, device_id=other, device_id_type=MESH
+    )
+
+
+def each(sizes, body):
+    total = 1
+    for size in sizes:
+        total *= size
+
+    def step(at, carry):
+        indices = []
+        for size in reversed(sizes):
+            indices.append(at % size)
+            at = at // size
+        body(*reversed(indices))
+        return carry
+
+    lax.fori_loop(0, total, step, 0)
+
+
+def pieces_of(rows):
+    size = min(rows, swap_rows)
+    return [(start, size) for start in range(0, rows, size)]
+
+
+def swap_steps(halves, outs, items, sems):
+    local, send, recv = sems
+    y = position()[3]
+    across_y = partners()[4]
+    pieces = [(i, *piece) for i, half in enumerate(halves) for piece in pieces_of(half.shape[1])]
+
+    def crossing(at):
+        i, start, size = pieces[at]
+        rows = pl.ds(start, size)
+        return remote(halves[i].at[1 - y, rows], items[i].at[y, rows], send.at[at], recv.at[at], across_y)
+
+    def keep(i):
+        return pltpu.make_async_copy(halves[i].at[y], items[i].at[y], local.at[i])
+
+    def ship(i):
+        return pltpu.make_async_copy(items[i], outs[i], local.at[i])
+
+    def begin(at):
+        crossing(at).start()
+        if pieces[at][1] == 0:
+            keep(pieces[at][0]).start()
+
+    def arrive():
+        for at in range(len(pieces)):
+            crossing(at).wait()
+        for i in range(len(halves)):
+            keep(i).wait()
+            ship(i).start()
+
+    def finish():
+        for i in range(len(halves)):
+            ship(i).wait()
+
+    return [functools.partial(begin, at) for at in range(len(pieces))], [arrive, finish]
+
+
+def peers_along(axis):
+    z, x, core, y = position()
+    *along, across_x, across_y, across_core = partners()
+    if axis == "z":
+        return [(other, (z + k + 1) % grid_z) for k, other in enumerate(along)]
+    return [{"x": (across_x, 1 - x), "y": (across_y, 1 - y), "c": (across_core, 1 - core)}[axis]]
+
+
+class LateSwap:
+    def __init__(self, values, item, sems, pieces):
+        local, send, recv = sems
+        y = position()[3]
+        half = values.shape[0] // 2
+        size = half // pieces
+
+        def crossing(at):
+            source = values.at[pl.ds(pl.multiple_of((1 - y) * half + at * size, size), size)]
+            return remote(source, item.at[y, pl.ds(at * size, size)], send.at[at], recv.at[at], partners()[4])
+
+        def keep():
+            return pltpu.make_async_copy(values.at[pl.ds(pl.multiple_of(y * half, half), half)], item.at[y], local.at[0])
+
+        self.crossing, self.keep, self.pieces = crossing, keep, pieces
+
+    def begin(self, at):
+        if at == 0:
+            self.keep().start()
+        self.crossing(at).start()
+
+    def finish(self):
+        self.keep().wait()
+        for at in range(self.pieces):
+            self.crossing(at).wait()
+
+
+def window(where):
+    row, rows, column, columns = where
+    return pl.ds(row, rows), pl.ds(column, columns)
+
+
+def gather_steps(groups, shards, outs, fulls, sems):
+    local, send, recv = sems
+    own_place = dict(zip("zxcy", position()))
+    chunks = [chunk for group in groups for chunk in group]
+    numbers = []
+    for group in groups:
+        start = numbers[-1][-1] + 1 if numbers else 0
+        numbers.append(list(range(start, start + len(group))))
+    first_sem = dict(zip("zxyc", (0, 3, 4, 5)))
+
+    def ref(i, hop):
+        weight, where, order = chunks[i]
+        at = [slice(None) if axis in order[:hop] else own_place[axis] for axis in "zxcy"]
+        return fulls[weight].at[(*at, *window(where))]
+
+    def source(i):
+        weight, where, _ = chunks[i]
+        return shards[weight].at[window(where)]
+
+    def keep(i):
+        return pltpu.make_async_copy(source(i), ref(i, 0), local.at[i])
+
+    def ship(i):
+        return pltpu.make_async_copy(ref(i, 4), outs[chunks[i][0]].at[(*[slice(None)] * 4, *window(chunks[i][1]))], local.at[i])
+
+    def hops(i, hop):
+        axis = chunks[i][2][hop]
+        where = first_sem[axis]
+        return [
+            remote(
+                source(i) if hop == 0 else ref(i, hop), ref(i, hop), send.at[i, where + k], recv.at[i, where + k], other
+            )
+            for k, (other, _) in enumerate(peers_along(axis))
+        ]
+
+    def begin():
+        for i in range(len(chunks)):
+            for copy in (keep(i), *hops(i, 0)):
+                copy.start()
+
+    def advance(step):
+        for hop in range(4):
+            if 0 <= step - hop * lag < len(groups):
+                for i in numbers[step - hop * lag]:
+                    if hop == 0:
+                        keep(i).wait()
+                    for copy in hops(i, hop):
+                        copy.wait_recv()
+                    if hop < 3:
+                        for copy in hops(i, hop + 1):
+                            copy.start()
+                    else:
+                        ship(i).start()
+
+    def finish():
+        for i in range(len(chunks)):
+            for hop in range(4):
+                for copy in hops(i, hop):
+                    copy.wait_send()
+            ship(i).wait()
+
+    return [begin, *(functools.partial(advance, step) for step in range(len(groups) + 3 * lag))], [finish]
+
+
+def scatter_steps(groups, grads, outs, buffers, sems):
+    mine, chip, *came = buffers
+    local, send, recv = sems
+    place = dict(zip("zxcy", position()))
+    sizes = dict(zip("zxy", (grid_z, grid_x, grid_y)))
+    first_sem = dict(zip("cxyz", (0, 1, 2, 3)))
+    chunks = [chunk for group in groups for chunk in group]
+    numbers = []
+    for group in groups:
+        start = numbers[-1][-1] + 1 if numbers else 0
+        numbers.append(list(range(start, start + len(group))))
+
+    def chip_hop(i):
+        weight, where, _ = chunks[i]
+        source = grads[weight].at[(slice(None), slice(None), 1 - place["c"], slice(None), *window(where))]
+        return remote(source, chip[i], send.at[i, 0], recv.at[i, 0], partners()[-1])
+
+    def keep(i):
+        weight, where, _ = chunks[i]
+        source = grads[weight].at[(slice(None), slice(None), place["c"], slice(None), *window(where))]
+        return pltpu.make_async_copy(source, mine[i], local.at[i])
+
+    def left(i, hop):
+        return [axis for axis in "zxy" if axis not in chunks[i][2][:hop]]
+
+    def held(i, hop):
+        return chip[i] if hop == 0 else came[hop - 1][i].at[0]
+
+    def hops(i, hop):
+        axis = chunks[i][2][hop]
+        copies = []
+        for k, (other, there) in enumerate(peers_along(axis)):
+            at = tuple(there if one == axis else slice(None) for one in left(i, hop))
+            where = first_sem[axis] + k
+            copies.append(
+                remote(held(i, hop).at[at], came[hop][i].at[k], send.at[i, where], recv.at[i, where], other)
+            )
+        return copies
+
+    def begin():
+        for i in range(len(chunks)):
+            chip_hop(i).start()
+        for i in range(min(kept_slots, len(chunks))):
+            keep(i).start()
+
+    def after_chip(i):
+        keep(i).wait()
+        chip_hop(i).wait_recv()
+
+        def add(*at):
+            chip[i][at] += mine[i][at]
+
+        each((grid_z, grid_x, grid_y), add)
+        for copy in hops(i, 0):
+            copy.start()
+        if i + kept_slots < len(chunks):
+            keep(i + kept_slots).start()
+
+    def after(i, hop):
+        weight, window_at, order = chunks[i]
+        for copy in hops(i, hop):
+            copy.wait_recv()
+        axis = order[hop]
+        before, rest = left(i, hop), left(i, hop + 1)
+        count = sizes[axis] - 1
+
+        def value(*at):
+            where = dict(zip(rest, at))
+            where[axis] = place[axis]
+            own = held(i, hop)[tuple(where[one] for one in before)]
+            if count == 1 and rest:
+                return own + came[hop][i][(0, *at)]
+            total = own.astype(jnp.float32)
+            for k in range(count):
+                total = total + came[hop][i][(k, *at)].astype(jnp.float32)
+            return total
+
+        if rest:
+
+            def add(*at):
+                came[hop][i][(0, *at)] = value(*at).astype(jnp.bfloat16)
+
+            each([sizes[one] for one in rest], add)
+            for copy in hops(i, hop + 1):
+                copy.start()
+        else:
+            outs[weight][window(window_at)] = value()
+
+    def advance(step):
+        for stage in range(4):
+            if 0 <= step - stage * lag < len(groups):
+                for i in numbers[step - stage * lag]:
+                    if stage == 0:
+                        after_chip(i)
+                    else:
+                        after(i, stage - 1)
+
+    def finish():
+        for i in range(len(chunks)):
+            for copy in (chip_hop(i), *(copy for hop in range(3) for copy in hops(i, hop))):
+                copy.wait_send()
+
+    return [begin, *(functools.partial(advance, step) for step in range(len(groups) + 3 * lag))], [finish]
+
+
+def reduce_steps(fill, total, came, send, recv, finish):
+    *along, across_x, across_y, across_core = partners()
+    singles = (across_core, across_x, across_y)
+
+    def single(k):
+        return remote(total.at[k], came.at[k], send.at[k], recv.at[k], singles[k])
+
+    def line(k):
+        return remote(total.at[3], came.at[3 + k], send.at[3 + k], recv.at[3 + k], along[k])
+
+    def begin():
+        fill()
+        single(0).start()
+
+    def add(k):
+        single(k).wait()
+        total[k + 1] = total[k] + came[k]
+        if k < 2:
+            single(k + 1).start()
+        else:
+            for j in range(grid_z - 1):
+                line(j).start()
+
+    def end():
+        value = total[3]
+        for j in range(grid_z - 1):
+            line(j).wait()
+            value = value + came[3 + j]
+        total[4] = value
+        finish()
+
+    return [begin, *(functools.partial(add, k) for k in range(3)), end]
+
+
+class Moves:
+    def __init__(self, gathers=(), gather_groups=(), scatters=(), scatter_groups=(), swaps=()):
+        blocks = grid_z * grid_x * grid_core * grid_y
+        self.gather_groups, self.scatter_groups = gather_groups, scatter_groups
+        gather_chunks = [chunk for group in gather_groups for chunk in group]
+        scatter_chunks = [chunk for group in scatter_groups for chunk in group]
+        self.scatter_count = len(scatter_chunks)
+        self.counts = (len(gathers), len(scatters), len(swaps))
+        views = [grad.reshape(block_grid + (grad.shape[0] // blocks, grad.shape[1])) for grad in scatters]
+        self.operands = [*gathers, *views, *swaps]
+        anywhere = pl.BlockSpec(memory_space=pl.ANY)
+        self.in_specs = [anywhere] * len(self.operands)
+        rows = [view.shape[-2:] for view in views]
+        self.out_specs = (
+            [anywhere] * len(gathers)
+            + [pl.BlockSpec(shape, lambda *at: (0, 0)) for shape in rows]
+            + [anywhere] * len(swaps)
+        )
+        self.out_shape = (
+            [jax.ShapeDtypeStruct(block_grid + shard.shape, shard.dtype) for shard in gathers]
+            + [jax.ShapeDtypeStruct(shape, jnp.float32) for shape in rows]
+            + [jax.ShapeDtypeStruct(values.shape, values.dtype) for values in swaps]
+        )
+        sizes = [where[1::2] for _, where, _ in scatter_chunks]
+        self.slots = {}
+        self.scratch_shapes = []
+        for i, size in enumerate(sizes):
+            if i < kept_slots or sizes[i - kept_slots] != size:
+                self.slots[i] = len(self.scratch_shapes)
+                self.scratch_shapes.append(pltpu.VMEM((4, 2, 2) + size, jnp.bfloat16))
+            else:
+                self.slots[i] = self.slots[i - kept_slots]
+        self.kept = len(self.scratch_shapes)
+        self.scratch_shapes += [pltpu.VMEM((4, 2, 2) + size, jnp.bfloat16) for size in sizes]
+        extents = dict(zip("zxy", (grid_z, grid_x, grid_y)))
+        for hop in range(3):
+            for (_, _, order), size in zip(scatter_chunks, sizes):
+                lead = [extents[order[hop]] - 1] + [extents[one] for one in "zxy" if one not in order[: hop + 1]]
+                self.scratch_shapes.append(pltpu.VMEM((*lead, *size), jnp.bfloat16))
+        self.scratch_shapes += [pltpu.VMEM(block_grid + shard.shape, shard.dtype) for shard in gathers]
+        self.scratch_shapes += [pltpu.VMEM(values.shape, values.dtype) for values in swaps]
+        for count, hops in ((len(gather_chunks), 6), (len(scatter_chunks), 6)):
+            if count:
+                self.scratch_shapes += [
+                    pltpu.SemaphoreType.DMA((count,)),
+                    pltpu.SemaphoreType.DMA((count, hops)),
+                    pltpu.SemaphoreType.DMA((count, hops)),
+                ]
+        if swaps:
+            pieces = sum(len(pieces_of(values.shape[1])) for values in swaps)
+            self.scratch_shapes += [pltpu.SemaphoreType.DMA((count,)) for count in (len(swaps), pieces, pieces)]
+
+    def steps(self, ins, outs, scratch):
+        gathers, scatters, swaps = self.counts
+        scratch = list(scratch)
+
+        def take(count):
+            taken = scratch[:count]
+            del scratch[:count]
+            return taken
+
+        kept = take(self.kept)
+        buffers = [[kept[self.slots[i]] for i in range(self.scatter_count)]]
+        buffers += [take(self.scatter_count) for _ in range(4)]
+        fulls, items = take(gathers), take(swaps)
+        lists = []
+        if gathers:
+            lists.append(gather_steps(self.gather_groups, ins[:gathers], outs[:gathers], fulls, take(3)))
+        if scatters:
+            span = slice(gathers, gathers + scatters)
+            lists.append(scatter_steps(self.scatter_groups, ins[span], outs[span], buffers, take(3)))
+        if swaps:
+            lists.append(swap_steps(ins[gathers + scatters :], outs[gathers + scatters :], items, take(3)))
+        steps = [meet]
+        for group in itertools.zip_longest(*(begin for begin, _ in lists)):
+            steps.append(functools.partial(call_all, [one for one in group if one is not None]))
+        steps[:2] = [functools.partial(call_all, steps[:2])]
+        ends = [end[0] for _, end in lists] + [one for _, end in lists for one in end[1:]]
+        steps.append(functools.partial(call_all, ends))
+        return steps
+
+
+def call_all(functions):
+    for function in functions:
+        function()
+
+
+def carried(body, moves, *, grid, in_specs, out_specs, out_shape, scratch_shapes, ident, name, last=None, tail=0):
+    if moves is None:
+        run = pl.pallas_call(
+            body,
+            grid=grid,
+            in_specs=in_specs,
+            out_specs=out_specs,
+            out_shape=out_shape,
+            scratch_shapes=scratch_shapes,
+            compiler_params=pltpu.CompilerParams(vmem_limit_bytes=48 * 1024 * 1024),
+            name=name,
+        )
+        return lambda *operands: (run(*operands), ())
+    counts = [len(in_specs), len(moves.in_specs), len(out_specs), len(moves.out_specs), len(scratch_shapes)]
+
+    def kernel(*refs):
+        refs = list(refs)
+        parts = []
+        for count in counts:
+            parts.append(refs[:count])
+            del refs[:count]
+        ins, move_ins, outs, move_outs, scratch = parts
+        steps = moves.steps(move_ins, move_outs, refs)
+        size = 1
+        for extent in grid:
+            size *= extent
+        at = pl.program_id(0)
+        early = len(steps) - tail
+        for i in range(size):
+            group = [steps[k] for k in range(early) if k * size // early == i]
+            if group:
+                pl.when(at == i)(functools.partial(call_all, group))
+        if body is not None:
+            body(*ins, *outs, *scratch)
+        late = [steps[early:]]
+        if last is not None:
+            late.append(last(*ins, *outs, *scratch))
+        order = [one for pairs in itertools.zip_longest(*late) for one in pairs if one is not None]
+        if order:
+            pl.when(at == size - 1)(functools.partial(call_all, order))
+
+    call = pl.pallas_call(
+        kernel,
+        grid=grid,
+        in_specs=[*in_specs, *moves.in_specs],
+        out_specs=[*out_specs, *moves.out_specs],
+        out_shape=[*out_shape, *moves.out_shape],
+        scratch_shapes=[*scratch_shapes, *moves.scratch_shapes],
+        compiler_params=pltpu.CompilerParams(
+            collective_id=ident, has_side_effects=True, vmem_limit_bytes=60 * 1024 * 1024
+        ),
+        name=name,
+    )
+
+    def run(*operands):
+        results = call(*operands, *moves.operands)
+        return results[: len(out_shape)], results[len(out_shape) :]
+
+    return run
+
+
+def cuts(weights, orders, most=24 * 384):
+    groups = []
+    for index, (rows, columns) in enumerate(weights):
+        if rows % 16 == 0:
+            pieces = [(row, 16, 0, columns) for row in range(0, rows, 16)]
+        else:
+            wide = max(most // rows // pair, 1) * pair
+            pieces = [(0, rows, column, min(wide, columns - column)) for column in range(0, columns, wide)]
+        for piece in pieces:
+            groups.append(((index, piece, orders[len(groups) % len(orders)]),))
+    return tuple(groups)
+
+
+def shard_shapes(grads):
+    blocks = grid_z * grid_x * grid_core * grid_y
+    return [(grad.shape[0] // blocks, grad.shape[1]) for grad in grads]
+
+
+def rms_backward(values, gain, grad):
+    scale = lax.rsqrt(jnp.mean(values * values, axis=-1, keepdims=True) + epsilon)
+    weighted = grad * gain
+    inner = jnp.mean(values * weighted, axis=-1, keepdims=True)
+    return scale * weighted - values * (scale * scale * scale * inner), jnp.sum(grad * values * scale, axis=0)
+
+
+def fits(mesh):
+    return mesh.shape["dp"] == grid_z * grid_x * grid_core and mesh.shape["seq"] == grid_y
+
+
+def item_body(
+    hidden,
+    encoded,
+    cotangent,
+    w_self_qkv,
+    w_self_out,
+    w_cross_q,
+    w_cross_kv,
+    w_cross_out,
+    w_ffn_in,
+    w_ffn_out,
+    norm_gains,
+    bucket_bias_matrix,
+    dec_lengths,
+    ident_tags,
+    ident_mask,
+    bucket_ids,
+):
+    width = hidden.shape[2]
+    heads = bucket_bias_matrix.shape[1]
+    bucket_count = bucket_bias_matrix.shape[0]
+    axes = ("dp", "seq")
+    place = lax.axis_index("seq")
+    both_ids = jnp.broadcast_to(bucket_ids.astype(jnp.bfloat16), (2,) + bucket_ids.shape)
+    lanes = (jnp.arange(pair) % (pair // 2) == 0).astype(jnp.float32)
+    tags = jnp.where(ident_tags[..., None] == 0, 0.0, masked_score * lanes).astype(jnp.bfloat16)
+    group = (w_self_qkv, w_cross_kv, w_self_out, w_cross_q, w_cross_out)
+    *weights, own_hidden, ids, tags, own_encoded = bring(
+        Moves(
+            group,
+            cuts([weight.shape for weight in group], ["yzxc"]),
+            swaps=[hidden, both_ids, tags, encoded],
+        )
+    )
+    tag_lanes = tags.reshape(-1, pair)
+    wqkv, wckv, wso, wcq, wco = (weight.reshape(width, -1) for weight in weights)
+    enc_rows = own_encoded.reshape(-1, width)
+    states = own_hidden.reshape(-1, width)
+    ids = ids.reshape(-1, ids.shape[-1])
+    length = jnp.broadcast_to(lax.dynamic_index_in_dim(dec_lengths, place, 0, keepdims=True), (8, pair))
+    marks = lax.dynamic_index_in_dim(ident_mask, place, 0, keepdims=False)
+    table = jnp.concatenate(
+        [
+            jnp.transpose(bucket_bias_matrix),
+            jnp.full((heads, pair - bucket_count), masked_score, jnp.float32),
+        ],
+        axis=1,
+    ).reshape(heads // 2, 2, pair)
+    mark_lanes = jnp.where(marks[:, None] == 1, 0.0, lanes[None, :]).astype(jnp.bfloat16)
+
+    group = (w_ffn_in, w_ffn_out)
+    kept, (slse, clse), (win, wout, own_cotangent) = attention_forward(
+        length, ids, tag_lanes, mark_lanes, table, norm_gains, states, wqkv, enc_rows, wso, wcq, wckv, wco,
+        Moves(group, cuts([weight.shape for weight in group], ["yzxc", "zxyc"]), swaps=[cotangent]),
+    )
+    win = win.reshape(width, -1)
+    wout = wout.reshape(-1, width)
+    grad_low = own_cotangent.reshape(-1, width)
+    grad_top = grad_low.astype(jnp.float32)
+    after_cross, normed_three = kept.x2, kept.n3
+    pre = matmul(normed_three, win)
+    act = smooth_gelu(pre).astype(jnp.bfloat16)
+    block_out = (after_cross + matmul(act, wout)).astype(jnp.bfloat16)
+
+    halves = (2, -1, width)
+    grad_wout = contract_rows(act, grad_low).astype(jnp.bfloat16)
+    grad_act = contract_cols(grad_low, wout)
+    grad_pre = jax.vjp(smooth_gelu, pre)[1](grad_act)[0].astype(jnp.bfloat16)
+    grad_win = contract_rows(normed_three, grad_pre).astype(jnp.bfloat16)
+    back, gain_three = rms_backward(after_cross, norm_gains[2], contract_cols(grad_pre, win))
+    grad_cross = grad_top + back
+    cross_low = grad_cross.astype(jnp.bfloat16)
+    grad_wco = contract_rows(kept.catt, cross_low).astype(jnp.bfloat16)
+    grad_catt = contract_cols(cross_low, wco).astype(jnp.bfloat16)
+    grads = [grad_wout, grad_win, grad_wco]
+    outs, (sum_wout, sum_win, sum_wco, block_out) = attention_backward(
+        kept.cq, kept.ckv, tag_lanes, mark_lanes, grad_catt, kept.cfull, clse,
+        kept.qkv, kept.ids_t, table, kept.sfull, slse,
+        norm_gains, states, kept.x1, grad_cross, kept.n1, kept.n2, kept.att, enc_rows,
+        wcq, wso, wckv, wqkv,
+        Moves(
+            scatters=grads,
+            scatter_groups=cuts(shard_shapes(grads), ["xzy", "xzy", "xzy", "yxz"]),
+            swaps=[block_out.reshape(halves)],
+        ),
+    )
+    grad_scores, grad_wqkv, grad_wckv, grad_wcq, grad_wso, grad_enc, grad_inputs, gain_rows = outs
+    gains = jnp.concatenate([gain_rows[0], gain_rows[1], gain_three])
+    rows = -(-gains.shape[0] // (8 * pair)) * 8
+    gains = jnp.pad(gains, (0, rows * pair - gains.shape[0])).reshape(rows, pair)
+    grads = [grad_wckv, grad_wcq, grad_wso, grad_wqkv]
+    (small,), (sum_wckv, sum_wcq, sum_wso, sum_wqkv) = table_sums(
+        gains,
+        kept.ids_t,
+        grad_scores,
+        bucket_count,
+        Moves(
+            scatters=grads,
+            scatter_groups=cuts(shard_shapes(grads), ["xzy", "yxz"]),
+        ),
+    )
+    results = deliver(
+        [block_out, grad_inputs, grad_enc, sum_wqkv, sum_wso, sum_wcq, sum_wckv, sum_wco, sum_win, sum_wout]
+    )
+    gains = small[:rows].reshape(-1)[: 3 * width].reshape(3, width)
+    grad_table = small[rows:, :heads]
+    return (*results, gains, grad_table)
+
+
 def solution(mesh):
     placed = (
         P("dp", "seq", None),
@@ -310,6 +1714,13 @@
         P("dp", None),
         P("seq", None),
     )
+
+    def body(*arrays):
+        items = arrays[0].shape[0]
+        if items == 2 and lax.axis_size("seq") == 2 and fits(mesh):
+            return item_body(*arrays)
+        return split_body(*arrays)
+
     return jax.shard_map(
         body,
         mesh=mesh,

time: 1660 us -> 386 us (0.23)
  waiting for transfers between devices: 1140 us -> 0 us
  Pallas kernels: 0 us -> 327 us
  matrix products: 241 us -> 33 us
  local copies, waits for them, and re-layouts: 144 us -> 13.4 us
  other arithmetic: 68.4 us -> 6.99 us
  blocking collectives: 40.7 us -> 0 us
    reduce_scatter x9 -> x0, waiting for transfers between devices: 718 us -> none  [the longest x1 139 us: body(): lax.psum_scatter(tiled[6], ('dp', 'seq'), scatter_dimension=0, tiled=True)]
    all_gather x9 -> x0, waiting for transfers between devices: 417 us -> none  [the longest x1 72.6 us: forward_pass(): all_ckv = lax.all_gather(local_ckv, 'seq', axis=1, tiled=True)]
    pallas_call x0 -> x5, Pallas kernels: none -> 327 us  [the longest x4 323 us: run(): results = call(*operands, *moves.operands)]
    dot_general x14 -> x0, matrix products: 130 us -> none  [the longest x2 28.9 us: attend_backward(): jnp.einsum('iqhe,ikhe->ihqk', grad_out, values, preferred_element_type=jn...]
    reshape x25 -> x2, local copies, waits for them, and re-layouts: 82.6 us -> 1.21 us  [the longest x1 0.61 us: item_body(): gains = small[:rows].reshape(-1)[:3 * width].reshape(3, width)]
    psum x1 -> x0, blocking collectives: 40.7 us -> none  [body(): lax.psum((jnp.stack([gain_one, gain_two, gain_three]), bias_gradient), ('...]
    dot_general x7 -> x3, matrix products: 42.5 us -> 11.2 us  [contract_rows(): lax.dot_general(left, right, (((0,), (0,)), ((), ())), preferred_element_...]
    reduce_sum x4 -> x1, other arithmetic: 29.3 us -> 1.74 us  [rms_backward(): jnp.mean(values * values, axis=-1, keepdims=True) + epsilon]
  transfers between devices with their start and end apart: 18 -> 0, of which waited for: 16 -> 0; matrix products, arithmetic and copies ran while one was open for 19% -> 0% of each run, Pallas kernels for 0% -> 0%
where the time goes in v1:
time: 386 us; the launch traced here: 381 us
  Pallas kernels  327 us (85%)
  matrix products  33 us (9%)
  local copies, waits for them, and re-layouts  13.4 us (3%)
  other arithmetic  6.99 us (2%)
    pallas_call x4, Pallas kernels, run(): results = call(*operands, *moves.operands)  323 us
    dot_general x2, matrix products, matmul(): return jnp.dot(left, right, preferred_element_type=jnp.float32)  12.1 us
    dot_general x3, matrix products, contract_rows(): lax.dot_general(left, right, (((0,), (0,)), ((), ())), preferred_element_...  11.2 us
    dot_general x3, matrix products, contract_cols(): lax.dot_general(left, right, (((1,), (1,)), ((), ())), preferred_element_...  9.69 us

profile of v1, /device:TPU:0, one launch (start us, length us, event | category | flops | bytes accessed | tf_op | source)
XLA Modules:
  0.0 381.1 jit_solution(2231232922053977932)
XLA Ops:
  0.6 1.2 dynamic_slice.10
  1.9 0.7 compare_reduce_fusion
  2.6 0.7 broadcast_compare_fusion
  3.3 1.2 broadcast_in_dim.50.refs_0_
  4.6 0.7 slice_reduce_fusion.2
  5.3 0.7 concatenate.6
  6.6 0.8 select_convert_fusion.1.refs_7_
  7.4 0.9 select_convert_fusion.refs_3_.refs_4_
  8.3 1.1 convert_element_type.45
  9.4 0.8 broadcast_in_dim.51.refs_6_
  10.2 71.3 %bring.1 = (bf16[4,2,2,2,24,2304]{5,4,3,2,1,0:T(8,128)(2,1)}, bf16[4,2,2,2,24,1536]{5,4,3,2,1,0:T(8,128)(2,1)}, bf16[4,2,2,2,24,768]{5,4,3,2,1,0:T(8,128)(2,1)},...) custom-call(bf16[24,2304]{1,0:T(8,128)(2,1)} %refs_0_.1, ...), custom_call_target="tpu_custom_call" | custom-call | tf_op jit(solution)/shard_map/bring/pallas_call | solution.py:1554
  81.5 84.2 %attention_forward.1 = (bf16[512,768]{1,0:T(8,128)(2,1)}, s32[512,512]{1,0:T(8,128)}, bf16[512,2304]{1,0:T(8,128)(2,1)}, bf16[512,768]{1,0:T(8,128)(2,1)}, f32[5...) custom-call(s32[8,128]{1,0:T(8,128)} %broadcast_in_dim.50.refs_0_, ...), custom_call_target="tpu_custom_call" | custom-call | tf_op jit(solution)/shard_map/attention_forward/pallas_call | solution.py:1554
  165.8 1.7 multiply_reduce_fusion.2
  167.6 5.1 %fusion.10 = f32[512,3072]{1,0:T(8,128)S(1)} fusion(bf16[512,768]{1,0:T(8,128)(2,1)} %bitcast.58, bf16[3072,768]{1,0:T(8,128)(2,1)} %bitcast.69), kind=kOutput, calls=%fused_computation.39 | convolution fusion | flops 2415919104 | bytes 11796480 | tf_op jit(solution)/shard_map/dot_general | solution.py:42
  172.7 7.4 %fusion.3 = (bf16[512,3072]{1,0:T(8,128)(2,1)S(1)}, f32[512,3072]{1,0:T(8,128)S(1)}) fusion(f32[512,3072]{1,0:T(8,128)S(1)} %fusion.10, bf16[512,768]{1,0:T(8,128)(2,1)S(1)} %copy-done.15, bf16[768,3072]{1,0:T(8,128)(2,1)S(1)} %bitcast.67), kind=kOutput, calls=%fused_computation.7 | convolution fusion | flops 2453667840 | bytes 21233664 | tf_op jit(solution)/shard_map/dot_general | solution.py:32
  180.1 4.7 %add_convert_fusion = bf16[512,768]{1,0:T(8,128)(2,1)} fusion(f32[512,768]{1,0:T(8,128)S(1)} %copy-done.11, bf16[3072,768]{1,0:T(8,128)(2,1)S(1)} %bitcast.72, f32[512,3072]{1,0:T(8,128)S(1)} %get-tuple-element.137), kind=kOutput, calls=%fused_computation.14 | convolution fusion | flops 2430861312 | bytes 13369344 | tf_op jit(solution)/shard_map/dot_general | solution.py:32
  184.9 2.8 multiply_reduce_fusion
  188.2 0.8 copy-done.12
  189.0 1.7 convolution_convert_fusion.3.refs_5_
  190.7 1.8 convolution_convert_fusion.2
  192.6 4.4 %convolution_convert_fusion = bf16[768,3072]{1,0:T(8,128)(2,1)} fusion(bf16[512,768]{1,0:T(8,128)(2,1)S(1)} %copy-done.15, bf16[512,3072]{1,0:T(8,128)(2,1)S(1)} %get-tuple-element.136), kind=kOutput, calls=%fused_computation.11 | convolution fusion | flops 2418278400 | bytes 8650752 | tf_op jit(solution)/shard_map/dot_general | solution.py:36
  196.9 5.0 %convolution_convert_fusion.1 = bf16[3072,768]{1,0:T(8,128)(2,1)} fusion(bf16[512,768]{1,0:T(8,128)(2,1)S(1)} %bitcast.59, f32[512,3072]{1,0:T(8,128)S(1)} %get-tuple-element.137), kind=kOutput, calls=%fused_computation.12 | convolution fusion | flops 2432434176 | bytes 11796480 | tf_op jit(solution)/shard_map/dot_general | solution.py:36
  201.9 108.8 %attention_backward.1 = (bf16[12,512,512]{2,1,0:T(8,128)(2,1)}, bf16[768,2304]{1,0:T(8,128)(2,1)}, bf16[768,1536]{1,0:T(8,128)(2,1)}, bf16[768,768]{1,0:T(8,128)...) custom-call(bf16[512,768]{1,0:T(8,128)(2,1)} %get-tuple-element.75.r, ...), custom_call_target="tpu_custom_call" | custom-call | tf_op jit(solution)/shard_map/attention_backward/pallas_call | solution.py:1554
  310.8 0.8 slice_reduce_fusion.1
  312.3 58.9 %table_sums.1 = (f32[56,128]{1,0:T(8,128)}, f32[24,1536]{1,0:T(8,128)}, f32[24,768]{1,0:T(8,128)}, f32[24,768]{1,0:T(8,128)}, f32[24,2304]{1,0:T(8,128)}) custom-call(f32[24,128]{1,0:T(8,128)} %fusion.8.refs_0_, s32[512,512]{1,0:T(8,128)} %get-tuple-element.85.refs_11_.refs_1_, bf16[12,512,512]{2,1,0:T(8,128)(2,1)} %get-tuple-element.97.refs_2_, ...), custom_call_target="tpu_custom_call" | custom-call | tf_op jit(solution)/shard_map/table_sums/pallas_call | solution.py:1554
  371.3 0.9 copy-done.5
  372.2 0.9 copy-done.6
  373.1 0.9 copy-done.8
  374.0 0.9 copy-done.9
  374.9 3.3 deliver.1
  378.2 0.7 slice.21
  378.9 0.7 slice.22
  (46 shorter events, 3.0 us)
Async XLA Ops:
  165.8 6.9 %slice-start = ((s8[4718592]{0:T(1024)(128)(4,1)}), s8[4194304]{0:T(1024)(128)(4,1)S(1)}, s32[]{:S(2)}) async-start(s8[4718592]{0:T(1024)(128)(4,1)} %bitcast.65), calls=%async_computation | async-start | bytes 8388608
  167.5 5.2 %slice-start.1 = ((s8[4718592]{0:T(1024)(128)(4,1)}), s8[524288]{0:T(1024)(128)(4,1)S(1)}, s32[]{:S(2)}) async-start(s8[4718592]{0:T(1024)(128)(4,1)} %bitcast.65), calls=%async_computation.1 | async-start | bytes 1048576
  167.5 5.2 %copy-start.15 = (bf16[512,768]{1,0:T(8,128)(2,1)S(1)}, bf16[512,768]{1,0:T(8,128)(2,1)}, u32[]{:S(2)}) copy-start(bf16[512,768]{1,0:T(8,128)(2,1)} %get-tuple-element.79) | copy-start | bytes 2359300
  167.5 12.6 %slice-start.2 = ((s8[4718592]{0:T(1024)(128)(4,1)}), s8[4194304]{0:T(1024)(128)(4,1)S(1)}, s32[]{:S(2)}) async-start(s8[4718592]{0:T(1024)(128)(4,1)} %bitcast.70), calls=%async_computation.2 | async-start | bytes 8388608
  172.7 7.4 %copy-start.11 = (f32[512,768]{1,0:T(8,128)S(1)}, f32[512,768]{1,0:T(8,128)}, u32[]{:S(2)}) copy-start(f32[512,768]{1,0:T(8,128)} %get-tuple-element.78) | copy-start | bytes 4718596
  172.7 7.4 %slice-start.3 = ((s8[4718592]{0:T(1024)(128)(4,1)}), s8[524288]{0:T(1024)(128)(4,1)S(1)}, s32[]{:S(2)}) async-start(s8[4718592]{0:T(1024)(128)(4,1)} %bitcast.70), calls=%async_computation.3 | async-start | bytes 1048576
  184.9 2.9 copy-start.14
  187.7 1.3 copy-start.12
  187.7 3.0 copy-start.13
  189.0 7.9 %copy-start.10 = (f32[512,768]{1,0:T(8,128)}, f32[512,768]{1,0:T(8,128)S(1)}, u32[]{:S(2)}) copy-start(f32[512,768]{1,0:T(8,128)S(1)} %subtract_add_fusion.refs_18_) | copy-start | bytes 4718596
  312.2 59.0 %copy-start = (bf16[2,512,768]{2,1,0:T(8,128)(2,1)S(1)}, bf16[2,512,768]{2,1,0:T(8,128)(2,1)}, u32[]{:S(2)}) copy-start(bf16[2,512,768]{2,1,0:T(8,128)(2,1)} %get-tuple-element.95.refs_2_) | copy-start | bytes 4718596
  312.2 59.0 %copy-start.1 = (bf16[2,256,768]{2,1,0:T(8,128)(2,1)S(1)}, bf16[2,256,768]{2,1,0:T(8,128)(2,1)}, u32[]{:S(2)}) copy-start(bf16[2,256,768]{2,1,0:T(8,128)(2,1)} %get-tuple-element.94.refs_1_) | copy-start | bytes 2359300
  312.2 59.0 %copy-start.2 = (bf16[2,256,768]{2,1,0:T(8,128)(2,1)S(1)}, bf16[2,256,768]{2,1,0:T(8,128)(2,1)}, u32[]{:S(2)}) copy-start(bf16[2,256,768]{2,1,0:T(8,128)(2,1)} %get-tuple-element.93.refs_0_) | copy-start | bytes 2359300
  312.2 59.0 %copy-start.3 = (f32[96,768]{1,0:T(8,128)S(1)}, f32[96,768]{1,0:T(8,128)}, u32[]{:S(2)}) copy-start(f32[96,768]{1,0:T(8,128)} %get-tuple-element.108.refs_9_) | copy-start | bytes 884740
  312.2 59.0 %copy-start.4 = (f32[24,3072]{1,0:T(8,128)S(1)}, f32[24,3072]{1,0:T(8,128)}, u32[]{:S(2)}) copy-start(f32[24,3072]{1,0:T(8,128)} %get-tuple-element.107.refs_8_) | copy-start | bytes 884740
  312.2 59.0 %copy-start.7 = (f32[24,768]{1,0:T(8,128)S(1)}, f32[24,768]{1,0:T(8,128)}, u32[]{:S(2)}) copy-start(f32[24,768]{1,0:T(8,128)} %get-tuple-element.106.refs_7_) | copy-start | bytes 221188
  371.3 0.9 copy-start.5
  372.2 0.9 copy-start.6
  373.1 0.9 copy-start.8
  374.0 0.9 copy-start.9

commit v2 on v1

--- a/solution.py
+++ b/solution.py
@@ -473,13 +473,14 @@
         for i in wanted:
             fetch(i).start()
         gain = given.gains[0:1, :]
+        length = jnp.where(lax.axis_index("seq") == 0, given.length[0:1, :], given.length[1:2, :])
         for start in range(0, rows, block):
             rest = slice(start, start + block)
             here.n1[rest, :] = rms_rows(given.x[rest, :].astype(jnp.float32), gain)
             for wide in range(0, rows, block):
                 query = lax.broadcasted_iota(jnp.int32, (block, block), 0) + start
                 key = lax.broadcasted_iota(jnp.int32, (block, block), 1) + wide
-                keep = (key <= query) & (key < given.length[0:1, :])
+                keep = (key <= query) & (key < length)
                 ids = given.ids[rest, wide : wide + block].astype(jnp.float32)
                 ids = jnp.where(keep, ids, float(masked_bucket))
                 masked[rest, wide : wide + block] = ids.astype(jnp.int32)
@@ -490,7 +491,7 @@
     @pl.when(at == 1)
     def _():
         for panel in range(3):
-            product_rows(here.n1, given.wqkv.at[:, columns(panel)], here.qkv.at[:, columns(panel)], 2 * block)
+            product_rows(here.n1, given.wqkv.at[:, columns(panel)], here.qkv.at[:, columns(panel)], 4 * block)
         ship(made.qkv).start()
 
     @pl.when((at > 1) & (at <= pairs + 1))
@@ -517,7 +518,7 @@
             total = given.x[rest, :].astype(jnp.float32) + matmul(here.att[rest, :], near.wso[...])
             here.x1[rest, :] = total
             here.n2[rest, :] = rms_rows(total, given.gains[1:2, :])
-        product_rows(here.n2, near.wcq, here.cq, 2 * block)
+        product_rows(here.n2, near.wcq, here.cq, 4 * block)
         for i in (made.att, made.sfull, made.x1, made.n2, made.cq):
             ship(i).start()
 
@@ -526,7 +527,7 @@
         fetch(wanted.enc).wait()
         fetch(wanted.wckv).wait()
         for panel in range(2):
-            product_rows(near.enc, near.wckv.at[:, columns(panel)], here.ckv.at[:, columns(panel)], 2 * block)
+            product_rows(near.enc, near.wckv.at[:, columns(panel)], here.ckv.at[:, columns(panel)], 4 * block)
         ship(made.ckv).start()
 
     @pl.when((at > pairs + 3) & (at <= 2 * pairs + 3))
@@ -637,8 +638,10 @@
         target[start : start + pair, :rows] = jnp.transpose(source[:, start : start + pair])
 
 
-def product_rows(left, right, target, block, dims=(((1,), (0,)), ((), ()))):
-    for start in range(0, target.shape[0], block):
+def product_rows(left, right, target, most, dims=(((1,), (0,)), ((), ()))):
+    rows = target.shape[0]
+    block = max(size for size in range(1, most + 1) if rows % size == 0)
+    for start in range(0, rows, block):
         here = slice(start, start + block)
         product = lax.dot_general(left[here, :], right[...], dims, preferred_element_type=jnp.float32)
         target[here, :] = product.astype(jnp.bfloat16)
@@ -722,14 +725,14 @@
     def _():
         gain = gains_ref[1:2, :]
         sums = None
-        for start in range(0, rows, block):
-            here = slice(start, start + block)
+        for start in range(0, rows, 2 * block):
+            here = slice(start, start + 2 * block)
             back, part = rms_back_rows(x1_ref[here, :], gain, nt(gcq[here, :], wcq_ref[...]))
             gx1[here, :] = gx2_ref[here, :] + back
             low_x1[here, :] = gx1[here, :].astype(jnp.bfloat16)
             sums = part if sums is None else sums + part
         ggain_ref[1:2, :] = sums
-        product_rows(low_x1, wso_ref, gatt, 2 * block, nt_dims)
+        product_rows(low_x1, wso_ref, gatt, 4 * block, nt_dims)
 
     enc_pieces, x_pieces = enc_sems[1].shape[0], x_sems[1].shape[0]
     enc_swap = LateSwap(genc, enc_items, enc_sems, enc_pieces)
@@ -737,7 +740,7 @@
 
     @pl.when(at == pairs + 1)
     def _():
-        product_rows(gckv, wckv_ref, genc, 2 * block, nt_dims)
+        product_rows(gckv, wckv_ref, genc, 4 * block, nt_dims)
 
     for piece in range(enc_pieces):
         pl.when(at == min(pairs + 2 + piece, 2 * pairs + 5))(functools.partial(enc_swap.begin, piece))
@@ -773,7 +776,7 @@
         @pl.when(at == 2 * pairs + 2 + panel)
         def _(panel=panel):
             columns = slice(panel * width, (panel + 1) * width)
-            product_rows(tall.at[:, :rows], gqkv.at[:, columns], gwqkv_ref, 2 * block)
+            product_rows(tall.at[:, :rows], gqkv.at[:, columns], gwqkv_ref, 4 * block)
             for start in range(0, rows, 2 * block):
                 here = slice(start, start + 2 * block)
                 part = nt(gqkv[here, columns], wqkv_ref[...])
@@ -797,14 +800,14 @@
         turn(enc_ref, tall)
         for panel in range(2):
             columns = slice(panel * width, (panel + 1) * width)
-            product_rows(tall.at[:, :keys], gckv.at[:, columns], gwckv_ref.at[:, columns], 2 * block)
+            product_rows(tall.at[:, :keys], gckv.at[:, columns], gwckv_ref.at[:, columns], 4 * block)
 
     @pl.when(at == 2 * pairs + 6)
     def _():
         turn(n2_ref, tall)
-        product_rows(tall.at[:, :rows], gcq, gwcq_ref, 2 * block)
+        product_rows(tall.at[:, :rows], gcq, gwcq_ref, 4 * block)
         turn(att_ref, tall)
-        product_rows(tall.at[:, :rows], low_x1, gwso_ref, 2 * block)
+        product_rows(tall.at[:, :rows], low_x1, gwso_ref, 4 * block)
         enc_swap.finish()
         x_swap.finish()
 
@@ -1625,7 +1628,7 @@
     enc_rows = own_encoded.reshape(-1, width)
     states = own_hidden.reshape(-1, width)
     ids = ids.reshape(-1, ids.shape[-1])
-    length = jnp.broadcast_to(lax.dynamic_index_in_dim(dec_lengths, place, 0, keepdims=True), (8, pair))
+    length = jnp.broadcast_to(dec_lengths[:, None], (2, pair))
     marks = lax.dynamic_index_in_dim(ident_mask, place, 0, keepdims=False)
     table = jnp.concatenate(
         [

time: 386 us -> 384 us (level)
  no operation moved by 1% of the time
where the time goes in v2:
time: 384 us; the launch traced here: 380 us
  Pallas kernels  326 us (85%)
  matrix products  33 us (9%)
  local copies, waits for them, and re-layouts  12.2 us (3%)
  other arithmetic  6.99 us (2%)
    pallas_call x4, Pallas kernels, run(): results = call(*operands, *moves.operands)  323 us
    dot_general x2, matrix products, matmul(): return jnp.dot(left, right, preferred_element_type=jnp.float32)  12.1 us
    dot_general x3, matrix products, contract_rows(): lax.dot_general(left, right, (((0,), (0,)), ((), ())), preferred_element_...  11.2 us
    dot_general x3, matrix products, contract_cols(): lax.dot_general(left, right, (((1,), (1,)), ((), ())), preferred_element_...  9.69 us

profile of v2, /device:TPU:0, one launch (start us, length us, event | category | flops | bytes accessed | tf_op | source)
XLA Modules:
  0.0 379.6 jit_solution(3690210327651502626)
XLA Ops:
  0.6 0.7 compare_reduce_fusion
  1.4 1.3 broadcast_in_dim.51.refs_0_
  2.7 0.7 broadcast_compare_fusion
  3.4 0.7 slice_reduce_fusion.2
  4.1 0.7 concatenate.6
  5.4 0.8 select_convert_fusion.1.refs_7_
  6.2 0.9 select_convert_fusion.refs_3_.refs_4_
  7.1 1.1 convert_element_type.45
  8.2 0.8 broadcast_in_dim.52.refs_6_
  9.0 71.3 %bring.1 = (bf16[4,2,2,2,24,2304]{5,4,3,2,1,0:T(8,128)(2,1)}, bf16[4,2,2,2,24,1536]{5,4,3,2,1,0:T(8,128)(2,1)}, bf16[4,2,2,2,24,768]{5,4,3,2,1,0:T(8,128)(2,1)},...) custom-call(bf16[24,2304]{1,0:T(8,128)(2,1)} %refs_0_.1, ...), custom_call_target="tpu_custom_call" | custom-call | tf_op jit(solution)/shard_map/bring/pallas_call | solution.py:1557
  80.3 84.3 %attention_forward.1 = (bf16[512,768]{1,0:T(8,128)(2,1)}, s32[512,512]{1,0:T(8,128)}, bf16[512,2304]{1,0:T(8,128)(2,1)}, bf16[512,768]{1,0:T(8,128)(2,1)}, f32[5...) custom-call(s32[2,128]{1,0:T(2,128)} %broadcast_in_dim.51.refs_0_, ...), custom_call_target="tpu_custom_call" | custom-call | tf_op jit(solution)/shard_map/attention_forward/pallas_call | solution.py:1557
  164.7 1.7 multiply_reduce_fusion.2
  166.4 5.1 %fusion.10 = f32[512,3072]{1,0:T(8,128)S(1)} fusion(bf16[512,768]{1,0:T(8,128)(2,1)} %bitcast.57, bf16[3072,768]{1,0:T(8,128)(2,1)} %bitcast.68), kind=kOutput, calls=%fused_computation.39 | convolution fusion | flops 2415919104 | bytes 11796480 | tf_op jit(solution)/shard_map/dot_general | solution.py:42
  171.6 7.4 %fusion.3 = (bf16[512,3072]{1,0:T(8,128)(2,1)S(1)}, f32[512,3072]{1,0:T(8,128)S(1)}) fusion(f32[512,3072]{1,0:T(8,128)S(1)} %fusion.10, bf16[512,768]{1,0:T(8,128)(2,1)S(1)} %copy-done.15, bf16[768,3072]{1,0:T(8,128)(2,1)S(1)} %bitcast.66), kind=kOutput, calls=%fused_computation.7 | convolution fusion | flops 2453667840 | bytes 21233664 | tf_op jit(solution)/shard_map/dot_general | solution.py:32
  179.1 4.7 %add_convert_fusion = bf16[512,768]{1,0:T(8,128)(2,1)} fusion(f32[512,768]{1,0:T(8,128)S(1)} %copy-done.11, bf16[3072,768]{1,0:T(8,128)(2,1)S(1)} %bitcast.71, f32[512,3072]{1,0:T(8,128)S(1)} %get-tuple-element.137), kind=kOutput, calls=%fused_computation.14 | convolution fusion | flops 2430861312 | bytes 13369344 | tf_op jit(solution)/shard_map/dot_general | solution.py:32
  183.8 2.8 multiply_reduce_fusion
  187.1 0.8 copy-done.12
  187.9 1.7 convolution_convert_fusion.3.refs_5_
  189.6 1.8 convolution_convert_fusion.2
  191.5 4.4 %convolution_convert_fusion = bf16[768,3072]{1,0:T(8,128)(2,1)} fusion(bf16[512,768]{1,0:T(8,128)(2,1)S(1)} %copy-done.15, bf16[512,3072]{1,0:T(8,128)(2,1)S(1)} %get-tuple-element.136), kind=kOutput, calls=%fused_computation.11 | convolution fusion | flops 2418278400 | bytes 8650752 | tf_op jit(solution)/shard_map/dot_general | solution.py:36
  195.8 5.0 %convolution_convert_fusion.1 = bf16[3072,768]{1,0:T(8,128)(2,1)} fusion(bf16[512,768]{1,0:T(8,128)(2,1)S(1)} %bitcast.58, f32[512,3072]{1,0:T(8,128)S(1)} %get-tuple-element.137), kind=kOutput, calls=%fused_computation.12 | convolution fusion | flops 2432434176 | bytes 11796480 | tf_op jit(solution)/shard_map/dot_general | solution.py:36
  200.9 109.1 %attention_backward.1 = (bf16[12,512,512]{2,1,0:T(8,128)(2,1)}, bf16[768,2304]{1,0:T(8,128)(2,1)}, bf16[768,1536]{1,0:T(8,128)(2,1)}, bf16[768,768]{1,0:T(8,128)...) custom-call(bf16[512,768]{1,0:T(8,128)(2,1)} %get-tuple-element.75.r, ...), custom_call_target="tpu_custom_call" | custom-call | tf_op jit(solution)/shard_map/attention_backward/pallas_call | solution.py:1557
  309.9 0.8 slice_reduce_fusion.1
  311.4 58.3 %table_sums.1 = (f32[56,128]{1,0:T(8,128)}, f32[24,1536]{1,0:T(8,128)}, f32[24,768]{1,0:T(8,128)}, f32[24,768]{1,0:T(8,128)}, f32[24,2304]{1,0:T(8,128)}) custom-call(f32[24,128]{1,0:T(8,128)} %fusion.8.refs_0_, s32[512,512]{1,0:T(8,128)} %get-tuple-element.85.refs_11_.refs_1_, bf16[12,512,512]{2,1,0:T(8,128)(2,1)} %get-tuple-element.97.refs_2_, ...), custom_call_target="tpu_custom_call" | custom-call | tf_op jit(solution)/shard_map/table_sums/pallas_call | solution.py:1557
  369.8 0.9 copy-done.5
  370.7 0.9 copy-done.6
  371.6 0.9 copy-done.8
  372.5 0.9 copy-done.9
  373.4 3.3 deliver.1
  376.7 0.7 slice.21
  377.4 0.7 slice.22
  378.1 0.7 copy.28
  (45 shorter events, 2.4 us)
Async XLA Ops:
  164.7 6.9 %slice-start = ((s8[4718592]{0:T(1024)(128)(4,1)}), s8[4194304]{0:T(1024)(128)(4,1)S(1)}, s32[]{:S(2)}) async-start(s8[4718592]{0:T(1024)(128)(4,1)} %bitcast.64), calls=%async_computation | async-start | bytes 8388608
  166.4 5.2 %slice-start.1 = ((s8[4718592]{0:T(1024)(128)(4,1)}), s8[524288]{0:T(1024)(128)(4,1)S(1)}, s32[]{:S(2)}) async-start(s8[4718592]{0:T(1024)(128)(4,1)} %bitcast.64), calls=%async_computation.1 | async-start | bytes 1048576
  166.4 5.2 %copy-start.15 = (bf16[512,768]{1,0:T(8,128)(2,1)S(1)}, bf16[512,768]{1,0:T(8,128)(2,1)}, u32[]{:S(2)}) copy-start(bf16[512,768]{1,0:T(8,128)(2,1)} %get-tuple-element.79) | copy-start | bytes 2359300
  166.4 12.6 %slice-start.2 = ((s8[4718592]{0:T(1024)(128)(4,1)}), s8[4194304]{0:T(1024)(128)(4,1)S(1)}, s32[]{:S(2)}) async-start(s8[4718592]{0:T(1024)(128)(4,1)} %bitcast.69), calls=%async_computation.2 | async-start | bytes 8388608
  171.6 7.4 %copy-start.11 = (f32[512,768]{1,0:T(8,128)S(1)}, f32[512,768]{1,0:T(8,128)}, u32[]{:S(2)}) copy-start(f32[512,768]{1,0:T(8,128)} %get-tuple-element.78) | copy-start | bytes 4718596
  171.6 7.4 %slice-start.3 = ((s8[4718592]{0:T(1024)(128)(4,1)}), s8[524288]{0:T(1024)(128)(4,1)S(1)}, s32[]{:S(2)}) async-start(s8[4718592]{0:T(1024)(128)(4,1)} %bitcast.69), calls=%async_computation.3 | async-start | bytes 1048576
  183.8 2.9 copy-start.14
  186.6 1.3 copy-start.12
  186.6 3.0 copy-start.13
  187.9 7.9 %copy-start.10 = (f32[512,768]{1,0:T(8,128)}, f32[512,768]{1,0:T(8,128)S(1)}, u32[]{:S(2)}) copy-start(f32[512,768]{1,0:T(8,128)S(1)} %subtract_add_fusion.refs_18_) | copy-start | bytes 4718596
  311.4 58.3 %copy-start = (bf16[2,512,768]{2,1,0:T(8,128)(2,1)S(1)}, bf16[2,512,768]{2,1,0:T(8,128)(2,1)}, u32[]{:S(2)}) copy-start(bf16[2,512,768]{2,1,0:T(8,128)(2,1)} %get-tuple-element.95.refs_2_) | copy-start | bytes 4718596
  311.4 58.4 %copy-start.1 = (bf16[2,256,768]{2,1,0:T(8,128)(2,1)S(1)}, bf16[2,256,768]{2,1,0:T(8,128)(2,1)}, u32[]{:S(2)}) copy-start(bf16[2,256,768]{2,1,0:T(8,128)(2,1)} %get-tuple-element.94.refs_1_) | copy-start | bytes 2359300
  311.4 58.4 %copy-start.2 = (bf16[2,256,768]{2,1,0:T(8,128)(2,1)S(1)}, bf16[2,256,768]{2,1,0:T(8,128)(2,1)}, u32[]{:S(2)}) copy-start(bf16[2,256,768]{2,1,0:T(8,128)(2,1)} %get-tuple-element.93.refs_0_) | copy-start | bytes 2359300
  311.4 58.4 %copy-start.3 = (f32[96,768]{1,0:T(8,128)S(1)}, f32[96,768]{1,0:T(8,128)}, u32[]{:S(2)}) copy-start(f32[96,768]{1,0:T(8,128)} %get-tuple-element.108.refs_9_) | copy-start | bytes 884740
  311.4 58.4 %copy-start.4 = (f32[24,3072]{1,0:T(8,128)S(1)}, f32[24,3072]{1,0:T(8,128)}, u32[]{:S(2)}) copy-start(f32[24,3072]{1,0:T(8,128)} %get-tuple-element.107.refs_8_) | copy-start | bytes 884740
  311.4 58.4 %copy-start.7 = (f32[24,768]{1,0:T(8,128)S(1)}, f32[24,768]{1,0:T(8,128)}, u32[]{:S(2)}) copy-start(f32[24,768]{1,0:T(8,128)} %get-tuple-element.106.refs_7_) | copy-start | bytes 221188
  369.8 0.9 copy-start.5
  370.7 0.9 copy-start.6
  371.6 0.9 copy-start.8
  372.5 0.9 copy-start.9
